TPU v7x, 32 devices: a whole 2x2x4 slice. The times are simulated.
32 devices in a mesh: seq: 8 (over z, y), head: 4 (over x, core).
Axes of the slice: x: 2, y: 2, z: 4, core: 2. Of those that a mesh axis runs over, the one named last changes fastest.
Arguments:
- inputs: bfloat16 [3, 2048, 1024], P(None, 'seq', 'head'), may hold values from -6 to 6
- memory: bfloat16 [3, 2048, 1024], P(None, 'seq', 'head'), may hold values from -6 to 6
- src_len: int32 [3, 2], replicated, may hold values from 128 to 1024, as said below
- w_query: bfloat16 [1024, 1024], P('seq', 'head'), may hold values from -0.1875 to 0.1875
- w_key: bfloat16 [1024, 1024], P('seq', 'head'), may hold values from -0.1875 to 0.1875
- w_value: bfloat16 [1024, 1024], P('seq', 'head'), may hold values from -0.1875 to 0.1875
- w_out: bfloat16 [1024, 1024], P('head', 'seq'), may hold values from -0.75 to 0.75
- c_query: bfloat16 [1024, 1024], P('seq', 'head'), may hold values from -0.1875 to 0.1875
- c_key: bfloat16 [1024, 1024], P('seq', 'head'), may hold values from -0.1875 to 0.1875
- c_value: bfloat16 [1024, 1024], P('seq', 'head'), may hold values from -0.1875 to 0.1875
- c_out: bfloat16 [1024, 1024], P('head', 'seq'), may hold values from -0.75 to 0.75
- ff_in: bfloat16 [1024, 4096], P('seq', 'head'), may hold values from -0.1875 to 0.1875
- ff_out: bfloat16 [4096, 1024], P('head', 'seq'), may hold values from -0.09375 to 0.09375
- prefix_self: bfloat16 [2, 30, 1024], P(None, None, 'head'), may hold values from -6 to 6
- prefix_cross: bfloat16 [2, 30, 1024], P(None, None, 'head'), may hold values from -6 to 6
- adapter_down: bfloat16 [1024, 512], P(None, 'head'), may hold values from -0.1875 to 0.1875
- down_bias: bfloat16 [512], P('head'), may hold values from -4 to 4
- adapter_up: bfloat16 [512, 1024], P('head'), may hold values from -0.0625 to 0.0625
- up_bias: bfloat16 [1024], P('head'), may hold values from -1 to 1
- cotangent: bfloat16 [3, 2048, 1024], P(None, 'seq', 'head'), may hold values from -6 to 6
Outputs:
- output: bfloat16 [3, 2048, 1024], P(None, 'seq', 'head')
- input_grad: bfloat16 [3, 2048, 1024], P(None, 'seq', 'head')
- memory_grad: bfloat16 [3, 2048, 1024], P(None, 'seq', 'head')
- prefix_self_grad: float32 [2, 30, 1024], P(None, None, 'head')
- prefix_cross_grad: float32 [2, 30, 1024], P(None, None, 'head')
- adapter_down_grad: float32 [1024, 512], P(None, 'head')
- down_bias_grad: float32 [512], P('head')
- adapter_up_grad: float32 [512, 1024], P('head')
- up_bias_grad: float32 [1024], P('head')
Inputs may be any that keep to these rules, and one draw needn't show every extreme that they name: `src_len`: in each micro-batch one row, drawn from the seed, has a source of all 1024 positions; the other rows have 1024 // 8 to 384.
All inputs are finite; a program needn't handle non-finite values.
Results may differ from a plain program's by a relative error of at most 0.033.
Values may be sent and summed in bfloat16 or wider, within the bound.
A program may use at most 80 MiB of HBM per device.

v0:
```python
import jax
import jax.numpy as jnp
from jax import lax
from jax.sharding import PartitionSpec as P

D = 1024
HD = 64
ROW = 1024


norm_epsilon = 1e-05


def from_partner(value, axis, stride):
    return lax.ppermute(value, axis, [(i, i ^ 1 << stride) for i in range(lax.axis_size(axis))])


def shortened(value):

    def short(part):
        return part.astype(jnp.bfloat16) if part.dtype == jnp.float32 else part

    return jax.tree.map(short, value)


def gelu_exact(values):
    return jax.nn.gelu(values, approximate=False)


def gelu_slope(values):
    return (
        0.5 * (1.0 + lax.erf(values * 0.7071067811865476))
        + values * jnp.exp(-0.5 * values * values) * 0.3989422804014327
    )


def token_time(positions, tok_rows, row_span):
    slot = positions // tok_rows
    inner = positions % tok_rows
    half = tok_rows // 2
    return jnp.where(
        inner < half, slot * half + inner, (2 * row_span - 1 - slot) * half + inner - half
    )


def features(shard_rows):
    return lax.all_gather(shard_rows, "head", axis=1, tiled=True)


def head_total(partial_sum):
    return lax.psum_scatter(
        partial_sum.astype(jnp.bfloat16), "head", scatter_dimension=1, tiled=True
    ).astype(jnp.float32)


def row_sums(left_term, right_term):
    return lax.psum((jnp.sum(left_term, axis=1), jnp.sum(right_term, axis=1)), "head")


def norm_forward(residual):
    row_total, square = row_sums(residual, residual * residual)
    center = row_total / D
    inverse = lax.rsqrt(square / D - center * center + norm_epsilon)
    return ((residual - center[:, None]) * inverse[:, None], inverse)


def norm_backward(normed, inverse, upstream):
    row_total, row_along = row_sums(upstream, upstream * normed)
    return inverse[:, None] * (upstream - row_total[:, None] / D - normed * row_along[:, None] / D)


def lower_side(section_bit):
    return lax.axis_index("seq") // (1 << section_bit) % 2 == 0


def join_halves(own_part, partner_part, section_bit):
    return jnp.where(
        lower_side(section_bit),
        jnp.concatenate([own_part, partner_part], axis=1),
        jnp.concatenate([partner_part, own_part], axis=1),
    )


def split_halves(key_grads, section_bit):
    half_rows = key_grads.shape[1] // 2
    lower_half = key_grads[:, :half_rows]
    upper_half = key_grads[:, half_rows:]
    keep_lower = lower_side(section_bit)
    return (
        jnp.where(keep_lower, lower_half, upper_half),
        jnp.where(keep_lower, upper_half, lower_half),
    )


def collect_self(stacked, sections):
    for section_bit in range(sections):
        stacked = join_halves(stacked, from_partner(stacked, "seq", section_bit), section_bit)
    return stacked


def collect_memory(stacked, sections):
    for section_bit in range(sections):
        stacked = join_halves(stacked, from_partner(stacked, "seq", section_bit), section_bit)
    return stacked


def return_self(key_grads, sections):
    for section_bit in reversed(range(sections)):
        own_part, sent_part = split_halves(key_grads, section_bit)
        key_grads = own_part + from_partner(
            sent_part.astype(jnp.bfloat16), "seq", section_bit
        ).astype(sent_part.dtype)
    return key_grads


def return_memory(key_grads, sections):
    for section_bit in reversed(range(sections)):
        own_part, sent_part = split_halves(key_grads, section_bit)
        key_grads = own_part + from_partner(
            sent_part.astype(jnp.bfloat16), "seq", section_bit
        ).astype(sent_part.dtype)
    return key_grads


def split_heads(matrix):
    return matrix.reshape(matrix.shape[0], -1, HD)


def score_block(queries, key_rows, pre_keys, visible):
    scores = jnp.einsum(
        "qhd,khd->hqk",
        split_heads(queries),
        split_heads(key_rows),
        preferred_element_type=jnp.float32,
    )
    scores = jnp.where(visible[None], scores, -1000000000.0)
    pre_scores = jnp.einsum(
        "qhd,khd->hqk",
        split_heads(queries),
        split_heads(pre_keys),
        preferred_element_type=jnp.float32,
    )
    return (scores, pre_scores)


def attend_forward(queries, key_rows, values, pre_keys, pre_values, visible):
    scores, pre_scores = score_block(queries, key_rows, pre_keys, visible)
    row_max = jnp.maximum(jnp.max(scores, axis=2), jnp.max(pre_scores, axis=2))
    exponents = jnp.exp(scores - row_max[:, :, None])
    pre_exponents = jnp.exp(pre_scores - row_max[:, :, None])
    row_total = jnp.sum(exponents, axis=2) + jnp.sum(pre_exponents, axis=2)
    log_total = row_max + jnp.log(row_total)
    weights = (exponents / row_total[:, :, None]).astype(jnp.bfloat16)
    pre_weights = (pre_exponents / row_total[:, :, None]).astype(jnp.bfloat16)
    mixed_out = jnp.einsum(
        "hqk,khd->qhd", weights, split_heads(values), preferred_element_type=jnp.float32
    )
    mixed_out = mixed_out + jnp.einsum(
        "hqk,khd->qhd", pre_weights, split_heads(pre_values), preferred_element_type=jnp.float32
    )
    return (mixed_out.reshape(queries.shape[0], -1).astype(jnp.bfloat16), log_total)


def attend_backward(
    queries, key_rows, values, pre_keys, pre_values, visible, log_total, grad_mixed
):
    scores, pre_scores = score_block(queries, key_rows, pre_keys, visible)
    weights = jnp.exp(scores - log_total[:, :, None])
    pre_weights = jnp.exp(pre_scores - log_total[:, :, None])
    grad_heads = split_heads(grad_mixed)
    query_heads = split_heads(queries)
    grad_weights = jnp.einsum(
        "qhd,khd->hqk", grad_heads, split_heads(values), preferred_element_type=jnp.float32
    )
    grad_pre = jnp.einsum(
        "qhd,khd->hqk", grad_heads, split_heads(pre_values), preferred_element_type=jnp.float32
    )
    row_delta = jnp.sum(weights * grad_weights, axis=2) + jnp.sum(pre_weights * grad_pre, axis=2)
    grad_scores = (weights * (grad_weights - row_delta[:, :, None])).astype(jnp.bfloat16)
    grad_pre_scores = (pre_weights * (grad_pre - row_delta[:, :, None])).astype(jnp.bfloat16)
    grad_queries = jnp.einsum(
        "hqk,khd->qhd", grad_scores, split_heads(key_rows), preferred_element_type=jnp.float32
    )
    grad_queries = grad_queries + jnp.einsum(
        "hqk,khd->qhd", grad_pre_scores, split_heads(pre_keys), preferred_element_type=jnp.float32
    )
    grad_queries = grad_queries.reshape(queries.shape[0], -1).astype(jnp.bfloat16)
    pre_count = pre_keys.shape[0]
    pre_key_grad = jnp.einsum(
        "hqk,qhd->khd", grad_pre_scores, query_heads, preferred_element_type=jnp.float32
    ).reshape(pre_count, -1)
    pre_value_grad = jnp.einsum(
        "hqk,qhd->khd",
        pre_weights.astype(jnp.bfloat16),
        grad_heads,
        preferred_element_type=jnp.float32,
    ).reshape(pre_count, -1)
    key_count = key_rows.shape[0]
    key_grad = jnp.einsum(
        "hqk,qhd->khd", grad_scores, query_heads, preferred_element_type=jnp.float32
    ).reshape(key_count, -1)
    value_grad = jnp.einsum(
        "hqk,qhd->khd", weights.astype(jnp.bfloat16), grad_heads, preferred_element_type=jnp.float32
    ).reshape(key_count, -1)
    return (
        grad_queries,
        jnp.stack([pre_key_grad, pre_value_grad]),
        jnp.stack([key_grad, value_grad]),
    )


def shards(
    inputs,
    memory,
    src_len,
    w_query,
    w_key,
    w_value,
    w_out,
    c_query,
    c_key,
    c_value,
    c_out,
    ff_in,
    ff_out,
    prefix_self,
    prefix_cross,
    adapter_down,
    down_bias,
    adapter_up,
    up_bias,
    cotangent,
):
    micro_count = inputs.shape[0]
    tok_rows = inputs.shape[1]
    source_dev = memory.shape[1]
    row_span = ROW // tok_rows
    sections = row_span.bit_length() - 1
    row_slot = lax.axis_index("seq") % row_span
    row_number = lax.axis_index("seq") // row_span
    query_time = token_time(row_slot * tok_rows + jnp.arange(tok_rows), tok_rows, row_span)
    key_time = token_time(jnp.arange(row_span * tok_rows), tok_rows, row_span)
    self_visible = key_time[None, :] <= query_time[:, None]
    source_positions = jnp.arange(row_span * source_dev)
    trained = (
        jnp.zeros(prefix_self.shape, jnp.float32),
        jnp.zeros(prefix_cross.shape, jnp.float32),
        jnp.zeros(adapter_down.shape, jnp.float32),
        jnp.zeros(down_bias.shape, jnp.float32),
        jnp.zeros(adapter_up.shape, jnp.float32),
        jnp.zeros(up_bias.shape, jnp.float32),
    )
    outputs = []
    input_grads = []
    memory_grads = []
    for micro_index in range(micro_count):
        frozen = (
            lax.all_gather(w_query, "seq", axis=0, tiled=True),
            lax.all_gather(w_key, "seq", axis=0, tiled=True),
            lax.all_gather(w_value, "seq", axis=0, tiled=True),
            lax.all_gather(c_query, "seq", axis=0, tiled=True),
            lax.all_gather(c_key, "seq", axis=0, tiled=True),
            lax.all_gather(c_value, "seq", axis=0, tiled=True),
            lax.all_gather(ff_in, "seq", axis=0, tiled=True),
            lax.all_gather(w_out, "seq", axis=1, tiled=True),
            lax.all_gather(c_out, "seq", axis=1, tiled=True),
            lax.all_gather(ff_out, "seq", axis=1, tiled=True),
        )
        (
            self_query,
            self_key,
            self_value,
            cross_query,
            cross_key,
            cross_value,
            hidden_in,
            self_out,
            cross_out,
            hidden_out,
        ) = frozen
        micro_rows = inputs[micro_index]
        whole_rows = features(micro_rows)
        queries = (
            jnp.dot(whole_rows, self_query, preferred_element_type=jnp.float32) * 0.125
        ).astype(jnp.bfloat16)
        key_own = jnp.dot(whole_rows, self_key, preferred_element_type=jnp.float32).astype(
            jnp.bfloat16
        )
        value_own = jnp.dot(whole_rows, self_value, preferred_element_type=jnp.float32).astype(
            jnp.bfloat16
        )
        self_gathered = collect_self(jnp.stack([key_own, value_own]), sections)
        key_rows, value_rows = (self_gathered[0], self_gathered[1])
        mixed_out, self_log = attend_forward(
            queries, key_rows, value_rows, prefix_self[0], prefix_self[1], self_visible
        )
        residual = micro_rows.astype(jnp.float32) + head_total(
            jnp.dot(mixed_out, self_out, preferred_element_type=jnp.float32)
        )
        first_norm, first_inverse = norm_forward(residual)
        first_whole = features(first_norm.astype(jnp.bfloat16))
        cross_queries = (
            jnp.dot(first_whole, cross_query, preferred_element_type=jnp.float32) * 0.125
        ).astype(jnp.bfloat16)
        memory_whole = features(memory[micro_index])
        memory_key_own = jnp.dot(
            memory_whole, cross_key, preferred_element_type=jnp.float32
        ).astype(jnp.bfloat16)
        memory_value_own = jnp.dot(
            memory_whole, cross_value, preferred_element_type=jnp.float32
        ).astype(jnp.bfloat16)
        memory_gathered = collect_memory(jnp.stack([memory_key_own, memory_value_own]), sections)
        memory_keys, memory_values = (memory_gathered[0], memory_gathered[1])
        cross_visible = (source_positions < src_len[micro_index][row_number])[None, :]
        cross_mixed, cross_log = attend_forward(
            cross_queries,
            memory_keys,
            memory_values,
            prefix_cross[0],
            prefix_cross[1],
            cross_visible,
        )
        residual = first_norm + head_total(
            jnp.dot(cross_mixed, cross_out, preferred_element_type=jnp.float32)
        )
        second, second_inverse = norm_forward(residual)
        second_whole = features(second.astype(jnp.bfloat16))
        hidden_pre = jnp.dot(second_whole, hidden_in, preferred_element_type=jnp.float32)
        hidden_low = gelu_exact(hidden_pre).astype(jnp.bfloat16)
        adapt_pre = jnp.dot(
            second_whole, adapter_down, preferred_element_type=jnp.float32
        ) + down_bias.astype(jnp.float32)
        adapt_low = gelu_exact(adapt_pre).astype(jnp.bfloat16)
        branch = jnp.dot(
            hidden_low, hidden_out, preferred_element_type=jnp.float32
        ) + 4.0 * jnp.dot(adapt_low, adapter_up, preferred_element_type=jnp.float32)
        residual = second + head_total(branch) + 4.0 * up_bias.astype(jnp.float32)
        third_norm, third_inverse = norm_forward(residual)
        outputs.append(third_norm.astype(jnp.bfloat16))
        grad_third = norm_backward(
            third_norm, third_inverse, cotangent[micro_index].astype(jnp.float32)
        )
        grad_branch = features(grad_third.astype(jnp.bfloat16))
        grad_hidden = (
            jnp.einsum("td,fd->tf", grad_branch, hidden_out, preferred_element_type=jnp.float32)
            * gelu_slope(hidden_pre)
        ).astype(jnp.bfloat16)
        grad_adapt = (
            4.0
            * jnp.einsum("td,ad->ta", grad_branch, adapter_up, preferred_element_type=jnp.float32)
            * gelu_slope(adapt_pre)
        ).astype(jnp.bfloat16)
        up_term = 4.0 * jnp.einsum(
            "ta,td->ad", adapt_low, grad_branch, preferred_element_type=jnp.float32
        )
        down_term = jnp.einsum(
            "td,ta->da", second_whole, grad_adapt, preferred_element_type=jnp.float32
        )
        down_bias_term = jnp.sum(grad_adapt.astype(jnp.float32), axis=0)
        up_bias_term = 4.0 * jnp.sum(grad_third, axis=0)
        back_second = jnp.einsum(
            "tf,df->td", grad_hidden, hidden_in, preferred_element_type=jnp.float32
        ) + jnp.einsum("ta,da->td", grad_adapt, adapter_down, preferred_element_type=jnp.float32)
        grad_second = grad_third + head_total(back_second)
        grad_residual = norm_backward(second, second_inverse, grad_second)
        grad_cross = features(grad_residual.astype(jnp.bfloat16))
        grad_cross_mixed = jnp.einsum(
            "td,ed->te", grad_cross, cross_out, preferred_element_type=jnp.float32
        ).astype(jnp.bfloat16)
        grad_cross_queries, cross_pre_term, cross_key_grads = attend_backward(
            cross_queries,
            memory_keys,
            memory_values,
            prefix_cross[0],
            prefix_cross[1],
            cross_visible,
            cross_log,
            grad_cross_mixed,
        )
        memory_summed = return_memory(cross_key_grads, sections).astype(jnp.bfloat16)
        memory_partial = jnp.einsum(
            "se,de->sd", memory_summed[0], cross_key, preferred_element_type=jnp.float32
        )
        memory_partial = memory_partial + jnp.einsum(
            "se,de->sd", memory_summed[1], cross_value, preferred_element_type=jnp.float32
        )
        memory_grads.append(head_total(memory_partial).astype(jnp.bfloat16))
        grad_first = grad_residual + head_total(
            0.125
            * jnp.einsum(
                "te,de->td", grad_cross_queries, cross_query, preferred_element_type=jnp.float32
            )
        )
        grad_residual = norm_backward(first_norm, first_inverse, grad_first)
        grad_self = features(grad_residual.astype(jnp.bfloat16))
        grad_mixed = jnp.einsum(
            "td,ed->te", grad_self, self_out, preferred_element_type=jnp.float32
        ).astype(jnp.bfloat16)
        grad_queries, self_pre_term, self_key_grads = attend_backward(
            queries,
            key_rows,
            value_rows,
            prefix_self[0],
            prefix_self[1],
            self_visible,
            self_log,
            grad_mixed,
        )
        self_summed = return_self(self_key_grads, sections).astype(jnp.bfloat16)
        input_partial = 0.125 * jnp.einsum(
            "te,de->td", grad_queries, self_query, preferred_element_type=jnp.float32
        )
        input_partial = input_partial + jnp.einsum(
            "te,de->td", self_summed[0], self_key, preferred_element_type=jnp.float32
        )
        input_partial = input_partial + jnp.einsum(
            "te,de->td", self_summed[1], self_value, preferred_element_type=jnp.float32
        )
        input_grads.append((grad_residual + head_total(input_partial)).astype(jnp.bfloat16))
        micro_terms = (
            self_pre_term,
            cross_pre_term,
            down_term,
            down_bias_term,
            up_term,
            up_bias_term,
        )
        trained = tuple(
            (held_sum + added_term for held_sum, added_term in zip(trained, micro_terms))
        )
    trained = jax.tree.map(
        lambda part: part.astype(jnp.float32), lax.psum(shortened(trained), "seq")
    )
    return (
        jnp.stack(outputs),
        jnp.stack(input_grads),
        jnp.stack(memory_grads),
        trained[0],
        trained[1],
        trained[2],
        trained[3],
        trained[4],
        trained[5],
    )


def solution(mesh):
    in_specs = (
        P(None, "seq", "head"),
        P(None, "seq", "head"),
        P(),
        P("seq", "head"),
        P("seq", "head"),
        P("seq", "head"),
        P("head", "seq"),
        P("seq", "head"),
        P("seq", "head"),
        P("seq", "head"),
        P("head", "seq"),
        P("seq", "head"),
        P("head", "seq"),
        P(None, None, "head"),
        P(None, None, "head"),
        P(None, "head"),
        P("head"),
        P("head", None),
        P("head"),
        P(None, "seq", "head"),
    )
    out_specs = (
        P(None, "seq", "head"),
        P(None, "seq", "head"),
        P(None, "seq", "head"),
        P(None, None, "head"),
        P(None, None, "head"),
        P(None, "head"),
        P("head"),
        P("head", None),
        P("head"),
    )
    return jax.shard_map(shards, mesh=mesh, in_specs=in_specs, out_specs=out_specs, check_vma=False)
```

profile of v0, /device:TPU:0, one launch (start us, length us, event | category | flops | bytes accessed | tf_op | source)
XLA Modules:
  0.0 1178.7 jit_solution(15787814818930893927)
XLA Ops:
  9.2 8.6 all-gather.4
  17.8 32.1 %all_gather.114 = bf16[1024,256]{1,0:T(8,128)(2,1)S(1)} all-gather(bf16[128,256]{1,0:T(8,128)(2,1)} %param.24), channel_id=1, replica_groups=mesh['seq'=8,'head'=4] {'seq'}, dimensions={0}, use_global_device_ids=true | all-gather | bytes 589824 | tf_op jit(solution)/shard_map/all_gather | solution.py:259
  50.0 31.5 %all_gather.115 = bf16[1024,256]{1,0:T(8,128)(2,1)S(1)} all-gather(bf16[128,256]{1,0:T(8,128)(2,1)} %param.25), channel_id=1, replica_groups=mesh['seq'=8,'head'=4] {'seq'}, dimensions={0}, use_global_device_ids=true | all-gather | bytes 589824 | tf_op jit(solution)/shard_map/all_gather | solution.py:260
  85.1 6.8 all-gather.3
  91.9 31.4 %all_gather.119 = bf16[1024,256]{1,0:T(8,128)(2,1)S(1)} all-gather(bf16[128,256]{1,0:T(8,128)(2,1)S(1)} %copy-done.174), channel_id=1, replica_groups=mesh['seq'=8,'head'=4] {'seq'}, dimensions={0}, use_global_device_ids=true | all-gather | bytes 589824 | tf_op jit(solution)/shard_map/all_gather | solution.py:262
  123.2 31.3 %all_gather.120 = bf16[1024,256]{1,0:T(8,128)(2,1)S(1)} all-gather(bf16[128,256]{1,0:T(8,128)(2,1)S(1)} %copy-done.175), channel_id=1, replica_groups=mesh['seq'=8,'head'=4] {'seq'}, dimensions={0}, use_global_device_ids=true | all-gather | bytes 589824 | tf_op jit(solution)/shard_map/all_gather | solution.py:263
  155.9 6.6 all-gather
  165.9 7.0 all-gather.2
  174.6 7.0 all-gather.5
  185.3 32.6 %all_gather.116 = bf16[1024,256]{1,0:T(8,128)(2,1)S(1)} all-gather(bf16[128,256]{1,0:T(8,128)(2,1)S(1)} %copy-done.176), channel_id=1, replica_groups=mesh['seq'=8,'head'=4] {'seq'}, dimensions={0}, use_global_device_ids=true | all-gather | bytes 589824 | tf_op jit(solution)/shard_map/all_gather | solution.py:258
  219.1 7.1 all-gather.1
  230.1 28.0 %all_gather.117 = bf16[256,1024]{1,0:T(8,128)(2,1)S(1)} all-gather(bf16[256,128]{1,0:T(8,128)(2,1)} %param.26), channel_id=1, replica_groups=mesh['seq'=8,'head'=4] {'seq'}, dimensions={1}, use_global_device_ids=true | all-gather | bytes 589824 | tf_op jit(solution)/shard_map/all_gather | solution.py:265
  258.1 31.5 %all_gather.122 = bf16[1024,256]{1,0:T(8,128)(2,1)S(1)} all-gather(bf16[128,256]{1,0:T(8,128)(2,1)} %param.27), channel_id=1, replica_groups=mesh['seq'=8,'head'=4] {'seq'}, dimensions={0}, use_global_device_ids=true | all-gather | bytes 589824 | tf_op jit(solution)/shard_map/all_gather | solution.py:261
  289.7 28.5 %all_gather.123 = bf16[256,1024]{1,0:T(8,128)(2,1)S(1)} all-gather(bf16[256,128]{1,0:T(8,128)(2,1)} %param.30), channel_id=1, replica_groups=mesh['seq'=8,'head'=4] {'seq'}, dimensions={1}, use_global_device_ids=true | all-gather | bytes 589824 | tf_op jit(solution)/shard_map/all_gather | solution.py:266
  346.2 10.0 collective-permute-done.1
  385.0 3.5 fusion.72
  407.8 16.3 %reduce-scatter.28.cloned.1.call-done = bf16[256,256]{1,0:T(8,128)(2,1)} async-done(((bf16[256,1024]{1,0:T(8,128)(2,1)}), bf16[256,256]{1,0:T(8,128)(2,1)}) %reduce-scatter.28.cloned.1.call-update) | async-done | bytes 131088 | tf_op jit(solution)/shard_map/reduce_scatter | solution.py:51
  424.1 24.2 %reduce-scatter.34.cloned.1.call-done = bf16[256,256]{1,0:T(8,128)(2,1)} async-done(((bf16[256,1024]{1,0:T(8,128)(2,1)}), bf16[256,256]{1,0:T(8,128)(2,1)}) %reduce-scatter.34.cloned.1.call-update) | async-done | bytes 131088 | tf_op jit(solution)/shard_map/reduce_scatter | solution.py:51
  450.2 6.5 all-reduce.5
  459.3 7.4 all_gather.129
  466.7 7.4 all_gather.133
  494.9 8.9 reduce-scatter.36.cloned.1.call-done
  503.8 24.6 %reduce-scatter.30.cloned.1.call-done = bf16[256,256]{1,0:T(8,128)(2,1)} async-done(((bf16[256,1024]{1,0:T(8,128)(2,1)}), bf16[256,256]{1,0:T(8,128)(2,1)}) %reduce-scatter.30.cloned.1.call-update) | async-done | bytes 131088 | tf_op jit(solution)/shard_map/reduce_scatter | solution.py:51
  530.5 6.8 all_gather.121
  544.1 20.5 %reduce-scatter.24.cloned.1.call-done = bf16[256,256]{1,0:T(8,128)(2,1)} async-done(((bf16[256,1024]{1,0:T(8,128)(2,1)}), bf16[256,256]{1,0:T(8,128)(2,1)}) %reduce-scatter.24.cloned.1.call-update) | async-done | bytes 131088 | tf_op jit(solution)/shard_map/reduce_scatter | solution.py:51
  566.4 6.5 all-reduce.4
  574.4 7.4 all_gather.124
  582.7 7.3 all_gather.130
  591.4 7.3 all_gather.134
  602.8 3.5 fusion.650
  606.4 39.2 %all-gather.11.cloned.1.call-done = bf16[1024,1024]{1,0:T(8,128)(2,1)} async-done(((bf16[1024,128]{1,0:T(8,128)(2,1)}), bf16[1024,1024]{1,0:T(8,128)(2,1)}) %all-gather.11.cloned.1.call-update) | async-done | bytes 2097168 | tf_op jit(solution)/shard_map/all_gather | solution.py:267
  645.5 4.7 fusion.196
  654.2 4.8 fusion.194
  662.9 4.7 fusion.192
  672.1 24.5 %reduce-scatter.32.cloned.1.call-done = bf16[256,256]{1,0:T(8,128)(2,1)} async-done(((bf16[256,1024]{1,0:T(8,128)(2,1)}), bf16[256,256]{1,0:T(8,128)(2,1)}) %reduce-scatter.32.cloned.1.call-update) | async-done | bytes 131088 | tf_op jit(solution)/shard_map/reduce_scatter | solution.py:51
  696.5 24.2 %reduce-scatter.38.cloned.1.call-done = bf16[256,256]{1,0:T(8,128)(2,1)} async-done(((bf16[256,1024]{1,0:T(8,128)(2,1)}), bf16[256,256]{1,0:T(8,128)(2,1)}) %reduce-scatter.38.cloned.1.call-update) | async-done | bytes 131088 | tf_op jit(solution)/shard_map/reduce_scatter | solution.py:51
  723.7 6.5 all-reduce.3
  734.5 6.5 all-reduce.2
  745.7 7.5 all_gather.135
  755.6 7.4 all_gather.138
  764.9 7.7 all_gather.141
  776.2 5.2 fusion.127
  783.9 5.2 fusion.128
  791.6 5.1 fusion.126
  802.3 46.6 %all-reduce.10.cloned.1.call-done = (bf16[1024,128]{1,0:T(8,128)(2,1)}, bf16[128,1024]{1,0:T(8,128)(2,1)}) async-done(((bf16[1024,128]{1,0:T(8,128)(2,1)}, bf16[128,1024]{1,0:T(8,128)(2,1)}), (bf16[1024,128]{1,0:T(8,128)(2,1)}, bf16[128,1024]{1,0:T(8,128)(2,1)})) %all-reduce.10.cloned.1.call-update) | async-done | bytes 524304 | tf_op jit(solution)/shard_map/psum | solution.py:432
  857.9 6.4 all-reduce.1
  867.0 7.4 all_gather.139
  879.6 7.3 all_gather.142
  889.2 7.6 all_gather.136
  921.7 4.2 multiply_convert_fusion.1
  931.3 5.1 multiply_convert_fusion.5
  963.7 3.8 collective-permute-done.21
  983.0 3.9 reduce-scatter.42.cloned.1.call-done
  988.6 6.0 all-reduce
  996.7 7.5 all_gather.140
  1006.5 7.4 all_gather.143
  1015.2 7.4 all_gather.137
  1031.2 5.7 multiply_reduce_fusion.4
  1037.0 6.9 multiply_convert_fusion.4
  1059.4 18.9 %collective-permute-done.12 = bf16[2,512,256]{1,2,0:T(8,128)(2,1)S(1)} collective-permute-done((bf16[2,512,256]{1,2,0:T(8,128)(2,1)S(1)}, bf16[2,512,256]{1,2,0:T(8,128)(2,1)S(1)}, u32[]{:S(2)}, u32[]{:S(2)}) %collective-permute-start.12) | collective-permute-done | bytes 524320 | tf_op jit(solution)/shard_map/ppermute | solution.py:15
  1080.9 8.1 collective-permute-done.16
  1092.2 4.9 collective-permute-done.17
  1114.5 38.7 %all-reduce.6 = (bf16[2,30,256]{2,1,0:T(8,128)(2,1)S(1)}, bf16[2,30,256]{2,1,0:T(8,128)(2,1)S(1)}, bf16[128]{0:T(256)(128)(2,1)S(1)}, bf16[256]{0:T(256)(128)(2,1)S(1)}) all-reduce(bf16[2,30,256]{2,1,0:T(8,128)(2,1)S(1)} %fusion.418, bf16[2,30,256]{2,1,0:T(8,128)(2,1)} %fusion.420, ...), channel_id=1, replica_groups=mesh['seq'=8,'head'=4] {'seq'}, use_global_device_ids=true, to_apply=%region_129.130 | all-reduce | flops 31104 | bytes 124416 | tf_op jit(solution)/shard_map/psum | solution.py:432
  1159.3 9.8 reduce-scatter.50.cloned.1.call-done
  (897 shorter events, 334.2 us)
Async XLA Ops:
  8.0 642.2 %copy-start = (bf16[128,1024]{1,0:T(8,128)(2,1)S(1)}, bf16[128,1024]{1,0:T(8,128)(2,1)}, u32[]{:S(2)}) copy-start(bf16[128,1024]{1,0:T(8,128)(2,1)} %param.37) | copy-start | bytes 786436
  8.0 76.4 %copy-start.157 = (bf16[3,256,256]{2,1,0:T(8,128)(2,1)S(1)}, bf16[3,256,256]{2,1,0:T(8,128)(2,1)}, u32[]{:S(2)}) copy-start(bf16[3,256,256]{2,1,0:T(8,128)(2,1)} %param.21) | copy-start | bytes 1179652
  8.0 83.8 %copy-start.174 = (bf16[128,256]{1,0:T(8,128)(2,1)S(1)}, bf16[128,256]{1,0:T(8,128)(2,1)}, u32[]{:S(2)}) copy-start(bf16[128,256]{1,0:T(8,128)(2,1)} %param.28) | copy-start | bytes 196612
  8.0 115.2 %copy-start.175 = (bf16[128,256]{1,0:T(8,128)(2,1)S(1)}, bf16[128,256]{1,0:T(8,128)(2,1)}, u32[]{:S(2)}) copy-start(bf16[128,256]{1,0:T(8,128)(2,1)} %param.29) | copy-start | bytes 196612
  8.1 399.8 %reduce-scatter.22.cloned.1.call-start = ((), (), s32[]{:S(2)}) async-start(), calls=%async_computation.21 | async-start | bytes 655360 | tf_op jit(solution)/shard_map/reduce_scatter | solution.py:51
  49.9 123.3 %copy-start.23 = (bf16[1024,256]{1,0:T(8,128)(2,1)}, bf16[1024,256]{1,0:T(8,128)(2,1)S(1)}, u32[]{:S(2)}) copy-start(bf16[1024,256]{1,0:T(8,128)(2,1)S(1)} %all_gather.114) | copy-start | bytes 1572868
  81.4 91.5 %copy-start.15 = (bf16[1024,256]{1,0:T(8,128)(2,1)}, bf16[1024,256]{1,0:T(8,128)(2,1)S(1)}, u32[]{:S(2)}) copy-start(bf16[1024,256]{1,0:T(8,128)(2,1)S(1)} %all_gather.115) | copy-start | bytes 1572868
  82.8 254.6 %collective-permute-start.8 = (bf16[2,256,256]{2,1,0:T(8,128)(2,1)}, bf16[2,256,256]{2,1,0:T(8,128)(2,1)}, u32[]{:S(2)}, u32[]{:S(2)}) collective-permute-start(bf16[2,256,256]{2,1,0:T(8,128)(2,1)} %pad_maximum_fusion.13), channel_id=1, source_target_pairs={{0,4},{4,0},{8,12},{12,8},{16,20},{20,16},{24,28},{28,24},{1,5},{5... | collective-permute-start | bytes 786440 | tf_op jit(solution)/shard_map/ppermute | solution.py:15
  123.2 103.3 %copy-start.21 = (bf16[1024,256]{1,0:T(8,128)(2,1)}, bf16[1024,256]{1,0:T(8,128)(2,1)S(1)}, u32[]{:S(2)}) copy-start(bf16[1024,256]{1,0:T(8,128)(2,1)S(1)} %all_gather.119) | copy-start | bytes 1572868
  155.9 234.1 %collective-permute-start.6 = (bf16[2,256,256]{2,1,0:T(8,128)(2,1)}, bf16[2,256,256]{2,1,0:T(8,128)(2,1)}, u32[]{:S(2)}, u32[]{:S(2)}) collective-permute-start(bf16[2,256,256]{2,1,0:T(8,128)(2,1)} %pad_maximum_fusion.12), channel_id=1, source_target_pairs={{0,4},{4,0},{8,12},{12,8},{16,20},{20,16},{24,28},{28,24},{1,5},{5... | collective-permute-start | bytes 786440 | tf_op jit(solution)/shard_map/ppermute | solution.py:15
  163.9 170.3 %collective-permute-start = (bf16[2,256,256]{2,1,0:T(8,128)(2,1)}, bf16[2,256,256]{2,1,0:T(8,128)(2,1)}, u32[]{:S(2)}, u32[]{:S(2)}) collective-permute-start(bf16[2,256,256]{2,1,0:T(8,128)(2,1)} %pad_maximum_fusion.9), channel_id=1, source_target_pairs={{0,4},{4,0},{8,12},{12,8},{16,20},{20,16},{24,28},{28,24},{1,5},{5... | collective-permute-start | bytes 786440 | tf_op jit(solution)/shard_map/ppermute | solution.py:15
  174.3 150.2 %collective-permute-start.4 = (bf16[2,256,256]{2,1,0:T(8,128)(2,1)}, bf16[2,256,256]{2,1,0:T(8,128)(2,1)}, u32[]{:S(2)}, u32[]{:S(2)}) collective-permute-start(bf16[2,256,256]{2,1,0:T(8,128)(2,1)} %pad_maximum_fusion.11), channel_id=1, source_target_pairs={{0,4},{4,0},{8,12},{12,8},{16,20},{20,16},{24,28},{28,24},{1,5},{5... | collective-permute-start | bytes 786440 | tf_op jit(solution)/shard_map/ppermute | solution.py:15
  183.0 149.3 %collective-permute-start.10 = (bf16[2,256,256]{2,1,0:T(8,128)(2,1)}, bf16[2,256,256]{2,1,0:T(8,128)(2,1)}, u32[]{:S(2)}, u32[]{:S(2)}) collective-permute-start(bf16[2,256,256]{2,1,0:T(8,128)(2,1)} %pad_maximum_fusion.14), channel_id=1, source_target_pairs={{0,4},{4,0},{8,12},{12,8},{16,20},{20,16},{24,28},{28,24},{1,5},{5... | collective-permute-start | bytes 786440 | tf_op jit(solution)/shard_map/ppermute | solution.py:15
  218.3 150.8 %copy-start.67 = (bf16[256,256]{0,1:T(8,128)(2,1)}, bf16[256,256]{0,1:T(8,128)(2,1)S(1)}, u32[]{:S(2)}) copy-start(bf16[256,256]{0,1:T(8,128)(2,1)S(1)} %fusion.106) | copy-start | bytes 393220
  218.7 152.2 %copy-start.64 = (bf16[256,256]{0,1:T(8,128)(2,1)}, bf16[256,256]{0,1:T(8,128)(2,1)S(1)}, u32[]{:S(2)}) copy-start(bf16[256,256]{0,1:T(8,128)(2,1)S(1)} %fusion.102) | copy-start | bytes 393220
  219.1 152.8 %copy-start.62 = (bf16[256,256]{0,1:T(8,128)(2,1)}, bf16[256,256]{0,1:T(8,128)(2,1)S(1)}, u32[]{:S(2)}) copy-start(bf16[256,256]{0,1:T(8,128)(2,1)S(1)} %fusion.104) | copy-start | bytes 393220
  219.1 105.4 %copy-start.131 = (bf16[1,256,256]{2,1,0:T(8,128)(2,1)S(1)}, bf16[1,256,256]{2,1,0:T(8,128)(2,1)}, u32[]{:S(2)}) copy-start(bf16[1,256,256]{2,1,0:T(8,128)(2,1)} %copy-done.130) | copy-start | bytes 393220
  219.1 105.4 %copy-start.133 = (bf16[1,256,256]{2,1,0:T(8,128)(2,1)S(1)}, bf16[1,256,256]{2,1,0:T(8,128)(2,1)}, u32[]{:S(2)}) copy-start(bf16[1,256,256]{2,1,0:T(8,128)(2,1)} %copy-done.132) | copy-start | bytes 393220
  226.6 97.9 %copy-start.122 = (bf16[1,256,256]{2,1,0:T(8,128)(2,1)}, bf16[1,256,256]{2,1,0:T(8,128)(2,1)S(1)}, u32[]{:S(2)}) copy-start(bf16[1,256,256]{2,1,0:T(8,128)(2,1)S(1)} %fusion.111) | copy-start | bytes 393220
  226.9 97.6 %copy-start.124 = (bf16[1,256,256]{2,1,0:T(8,128)(2,1)}, bf16[1,256,256]{2,1,0:T(8,128)(2,1)S(1)}, u32[]{:S(2)}) copy-start(bf16[1,256,256]{2,1,0:T(8,128)(2,1)S(1)} %fusion.110) | copy-start | bytes 393220
  228.6 95.9 %copy-start.113 = (bf16[30,4,64]{2,1,0:T(4,128)(2,1)}, bf16[30,4,64]{2,1,0:T(4,128)(2,1)S(1)}, u32[]{:S(2)}) copy-start(bf16[30,4,64]{2,1,0:T(4,128)(2,1)S(1)} %reshape_squeeze.34) | copy-start | bytes 46084
  325.7 15.0 %collective-permute-start.5 = (bf16[2,512,256]{2,1,0:T(8,128)(2,1)S(1)}, bf16[2,512,256]{2,1,0:T(8,128)(2,1)}, u32[]{:S(2)}, u32[]{:S(2)}) collective-permute-start(bf16[2,512,256]{2,1,0:T(8,128)(2,1)S(1)} %maximum_select_fusion.8), channel_id=1, source_target_pairs={{0,8},{4,12},{8,0},{12,4},{16,24},{20,28},{24,16},{28,20},{1,9},{5... | collective-permute-start | bytes 1572872 | tf_op jit(solution)/shard_map/ppermute | solution.py:15
  332.2 60.8 %collective-permute-start.2 = (bf16[2,256,256]{2,1,0:T(8,128)(2,1)}, bf16[2,256,256]{2,1,0:T(8,128)(2,1)}, u32[]{:S(2)}, u32[]{:S(2)}) collective-permute-start(bf16[2,256,256]{2,1,0:T(8,128)(2,1)} %pad_maximum_fusion.10), channel_id=1, source_target_pairs={{0,4},{4,0},{8,12},{12,8},{16,20},{20,16},{24,28},{28,24},{1,5},{5... | collective-permute-start | bytes 786440 | tf_op jit(solution)/shard_map/ppermute | solution.py:15
  334.2 61.1 %collective-permute-start.11 = (bf16[2,512,256]{2,1,0:T(8,128)(2,1)}, bf16[2,512,256]{2,1,0:T(8,128)(2,1)}, u32[]{:S(2)}, u32[]{:S(2)}) collective-permute-start(bf16[2,512,256]{2,1,0:T(8,128)(2,1)} %maximum_select_fusion.11), channel_id=1, source_target_pairs={{0,8},{4,12},{8,0},{12,4},{16,24},{20,28},{24,16},{28,20},{1,9},{5... | collective-permute-start | bytes 1572872 | tf_op jit(solution)/shard_map/ppermute | solution.py:15
  337.4 18.8 %collective-permute-start.1 = (bf16[2,512,256]{2,1,0:T(8,128)(2,1)S(1)}, bf16[2,512,256]{2,1,0:T(8,128)(2,1)}, u32[]{:S(2)}, u32[]{:S(2)}) collective-permute-start(bf16[2,512,256]{2,1,0:T(8,128)(2,1)S(1)} %maximum_select_fusion.6), channel_id=1, source_target_pairs={{0,8},{4,12},{8,0},{12,4},{16,24},{20,28},{24,16},{28,20},{1,9},{5... | collective-permute-start | bytes 1572872 | tf_op jit(solution)/shard_map/ppermute | solution.py:15
  340.8 21.4 %collective-permute-start.9 = (bf16[2,512,256]{2,1,0:T(8,128)(2,1)}, bf16[2,512,256]{2,1,0:T(8,128)(2,1)}, u32[]{:S(2)}, u32[]{:S(2)}) collective-permute-start(bf16[2,512,256]{2,1,0:T(8,128)(2,1)} %maximum_select_fusion.10), channel_id=1, source_target_pairs={{0,8},{4,12},{8,0},{12,4},{16,24},{20,28},{24,16},{28,20},{1,9},{5... | collective-permute-start | bytes 1572872 | tf_op jit(solution)/shard_map/ppermute | solution.py:15
  378.9 45.2 %reduce-scatter.28.cloned.1.call-start = ((), (), s32[]{:S(2)}) async-start(), calls=%async_computation.26 | async-start | bytes 655360 | tf_op jit(solution)/shard_map/reduce_scatter | solution.py:51
  384.4 63.9 %reduce-scatter.34.cloned.1.call-start = ((), (), s32[]{:S(2)}) async-start(), calls=%async_computation.29 | async-start | bytes 655360 | tf_op jit(solution)/shard_map/reduce_scatter | solution.py:51
  389.9 113.9 %reduce-scatter.36.cloned.1.call-start = ((), (), s32[]{:S(2)}) async-start(), calls=%async_computation.30 | async-start | bytes 655360 | tf_op jit(solution)/shard_map/reduce_scatter | solution.py:51
  391.2 10.6 collective-permute-start.7
  395.1 92.6 %collective-permute-start.3 = (bf16[2,512,256]{2,1,0:T(8,128)(2,1)}, bf16[2,512,256]{2,1,0:T(8,128)(2,1)}, u32[]{:S(2)}, u32[]{:S(2)}) collective-permute-start(bf16[2,512,256]{2,1,0:T(8,128)(2,1)} %maximum_select_fusion.7), channel_id=1, source_target_pairs={{0,8},{4,12},{8,0},{12,4},{16,24},{20,28},{24,16},{28,20},{1,9},{5... | collective-permute-start | bytes 1572872 | tf_op jit(solution)/shard_map/ppermute | solution.py:15
  399.6 76.9 %copy-start.56 = (bf16[1,1024,256]{1,2,0:T(8,128)(2,1)}, bf16[1,1024,256]{1,2,0:T(8,128)(2,1)S(1)}, u32[]{:S(2)}) copy-start(bf16[1,1024,256]{1,2,0:T(8,128)(2,1)S(1)} %copy.74) | copy-start | bytes 1572868
  481.7 46.8 %reduce-scatter.30.cloned.1.call-start = ((), (), s32[]{:S(2)}) async-start(), calls=%async_computation.27 | async-start | bytes 655360 | tf_op jit(solution)/shard_map/reduce_scatter | solution.py:51
  486.2 78.4 %reduce-scatter.24.cloned.1.call-start = ((), (), s32[]{:S(2)}) async-start(), calls=%async_computation.22 | async-start | bytes 655360 | tf_op jit(solution)/shard_map/reduce_scatter | solution.py:51
  542.4 60.5 %all-gather.9.cloned.1.call-start = ((), (), s32[]{:S(2)}) async-start(), calls=%async_computation.23 | async-start | bytes 2359296 | tf_op jit(solution)/shard_map/all_gather | solution.py:264
  542.9 102.6 %all-gather.11.cloned.1.call-start = ((), (), s32[]{:S(2)}) async-start(), calls=%async_computation.24 | async-start | bytes 2359296 | tf_op jit(solution)/shard_map/all_gather | solution.py:267
  543.5 128.6 %reduce-scatter.26.cloned.1.call-start = ((), (), s32[]{:S(2)}) async-start(), calls=%async_computation.25 | async-start | bytes 655360 | tf_op jit(solution)/shard_map/reduce_scatter | solution.py:51
  651.6 44.9 %reduce-scatter.32.cloned.1.call-start = ((), (), s32[]{:S(2)}) async-start(), calls=%async_computation.28 | async-start | bytes 655360 | tf_op jit(solution)/shard_map/reduce_scatter | solution.py:51
  660.3 60.4 %reduce-scatter.38.cloned.1.call-start = ((), (), s32[]{:S(2)}) async-start(), calls=%async_computation.31 | async-start | bytes 655360 | tf_op jit(solution)/shard_map/reduce_scatter | solution.py:51
  669.0 179.9 %all-reduce.10.cloned.1.call-start = ((), (), s32[]{:S(2)}) async-start(), calls=%async_computation.44 | async-start | bytes 1048576 | tf_op jit(solution)/shard_map/psum | solution.py:432
  776.1 76.4 %reduce-scatter.46.cloned.1.call-start = ((), (), s32[]{:S(2)}) async-start(), calls=%async_computation.35 | async-start | bytes 655360 | tf_op jit(solution)/shard_map/reduce_scatter | solution.py:51
  783.9 70.5 %reduce-scatter.40.cloned.1.call-start = ((), (), s32[]{:S(2)}) async-start(), calls=%async_computation.32 | async-start | bytes 655360 | tf_op jit(solution)/shard_map/reduce_scatter | solution.py:51
  791.5 64.6 %reduce-scatter.52.cloned.1.call-start = ((), (), s32[]{:S(2)}) async-start(), calls=%async_computation.38 | async-start | bytes 655360 | tf_op jit(solution)/shard_map/reduce_scatter | solution.py:51
  799.2 183.8 %reduce-scatter.48.cloned.1.call-start = ((), (), s32[]{:S(2)}) async-start(), calls=%async_computation.36 | async-start | bytes 655360 | tf_op jit(solution)/shard_map/reduce_scatter | solution.py:51
  918.2 64.8 %reduce-scatter.54.cloned.1.call-start = ((), (), s32[]{:S(2)}) async-start(), calls=%async_computation.39 | async-start | bytes 655360 | tf_op jit(solution)/shard_map/reduce_scatter | solution.py:51
  920.7 36.0 %collective-permute-start.20 = (bf16[2,512,256]{1,2,0:T(8,128)(2,1)}, bf16[2,512,256]{1,2,0:T(8,128)(2,1)}, u32[]{:S(2)}, u32[]{:S(2)}) collective-permute-start(bf16[2,512,256]{1,2,0:T(8,128)(2,1)} %select_convert_fusion.1), channel_id=1, source_target_pairs={{0,8},{4,12},{8,0},{12,4},{16,24},{20,28},{24,16},{28,20},{1,9},{5... | collective-permute-start | bytes 1572872 | tf_op jit(solution)/shard_map/ppermute | solution.py:15
  928.4 31.8 %collective-permute-start.22 = (bf16[2,512,256]{1,2,0:T(8,128)(2,1)}, bf16[2,512,256]{1,2,0:T(8,128)(2,1)}, u32[]{:S(2)}, u32[]{:S(2)}) collective-permute-start(bf16[2,512,256]{1,2,0:T(8,128)(2,1)} %select_convert_fusion), channel_id=1, source_target_pairs={{0,8},{4,12},{8,0},{12,4},{16,24},{20,28},{24,16},{28,20},{1,9},{5... | collective-permute-start | bytes 1572872 | tf_op jit(solution)/shard_map/ppermute | solution.py:15
  936.5 50.5 %reduce-scatter.42.cloned.1.call-start = ((), (), s32[]{:S(2)}) async-start(), calls=%async_computation.33 | async-start | bytes 655360 | tf_op jit(solution)/shard_map/reduce_scatter | solution.py:51
  955.6 13.9 %collective-permute-start.18 = (bf16[2,512,256]{1,2,0:T(8,128)(2,1)}, bf16[2,512,256]{1,2,0:T(8,128)(2,1)}, u32[]{:S(2)}, u32[]{:S(2)}) collective-permute-start(bf16[2,512,256]{1,2,0:T(8,128)(2,1)} %select_convert_fusion.2), channel_id=1, source_target_pairs={{0,8},{4,12},{8,0},{12,4},{16,24},{20,28},{24,16},{28,20},{1,9},{5... | collective-permute-start | bytes 1572872 | tf_op jit(solution)/shard_map/ppermute | solution.py:15
  956.6 198.9 %reduce-scatter.60.cloned.1.call-start = ((), (), s32[]{:S(2)}) async-start(), calls=%async_computation.42 | async-start | bytes 655360 | tf_op jit(solution)/shard_map/reduce_scatter | solution.py:51
  958.5 9.0 collective-permute-start.21
  963.2 11.4 collective-permute-start.23
  969.2 186.4 %reduce-scatter.62.cloned.1.call-start = ((), (), s32[]{:S(2)}) async-start(), calls=%async_computation.43 | async-start | bytes 655360 | tf_op jit(solution)/shard_map/reduce_scatter | solution.py:51
  973.0 7.3 collective-permute-start.19
  977.2 178.3 %reduce-scatter.58.cloned.1.call-start = ((), (), s32[]{:S(2)}) async-start(), calls=%async_computation.41 | async-start | bytes 655360 | tf_op jit(solution)/shard_map/reduce_scatter | solution.py:51
  982.9 174.5 %reduce-scatter.56.cloned.1.call-start = ((), (), s32[]{:S(2)}) async-start(), calls=%async_computation.40 | async-start | bytes 655360 | tf_op jit(solution)/shard_map/reduce_scatter | solution.py:51
  1052.3 38.6 %collective-permute-start.14 = (bf16[2,512,256]{1,2,0:T(8,128)(2,1)S(1)}, bf16[2,512,256]{1,2,0:T(8,128)(2,1)S(1)}, u32[]{:S(2)}, u32[]{:S(2)}) collective-permute-start(bf16[2,512,256]{1,2,0:T(8,128)(2,1)S(1)} %select_convert_fusion.4), channel_id=1, source_target_pairs={{0,8},{4,12},{8,0},{12,4},{16,24},{20,28},{24,16},{28,20},{1,9},{5... | collective-permute-start | bytes 1572872 | tf_op jit(solution)/shard_map/ppermute | solution.py:15
  1054.0 24.3 %collective-permute-start.12 = (bf16[2,512,256]{1,2,0:T(8,128)(2,1)S(1)}, bf16[2,512,256]{1,2,0:T(8,128)(2,1)S(1)}, u32[]{:S(2)}, u32[]{:S(2)}) collective-permute-start(bf16[2,512,256]{1,2,0:T(8,128)(2,1)S(1)} %select_convert_fusion.5), channel_id=1, source_target_pairs={{0,8},{4,12},{8,0},{12,4},{16,24},{20,28},{24,16},{28,20},{1,9},{5... | collective-permute-start | bytes 1572872 | tf_op jit(solution)/shard_map/ppermute | solution.py:15
  1054.8 34.2 %collective-permute-start.16 = (bf16[2,512,256]{1,2,0:T(8,128)(2,1)S(1)}, bf16[2,512,256]{1,2,0:T(8,128)(2,1)S(1)}, u32[]{:S(2)}, u32[]{:S(2)}) collective-permute-start(bf16[2,512,256]{1,2,0:T(8,128)(2,1)S(1)} %select_convert_fusion.3), channel_id=1, source_target_pairs={{0,8},{4,12},{8,0},{12,4},{16,24},{20,28},{24,16},{28,20},{1,9},{5... | collective-permute-start | bytes 1572872 | tf_op jit(solution)/shard_map/ppermute | solution.py:15
  1079.4 21.7 %collective-permute-start.13 = (bf16[2,256,256]{1,2,0:T(8,128)(2,1)}, bf16[2,256,256]{1,2,0:T(8,128)(2,1)}, u32[]{:S(2)}, u32[]{:S(2)}) collective-permute-start(bf16[2,256,256]{1,2,0:T(8,128)(2,1)} %select_convert_fusion.11), channel_id=1, source_target_pairs={{0,4},{4,0},{8,12},{12,8},{16,20},{20,16},{24,28},{28,24},{1,5},{5... | collective-permute-start | bytes 786440 | tf_op jit(solution)/shard_map/ppermute | solution.py:15
  1089.3 7.8 collective-permute-start.17
  1098.8 59.6 %reduce-scatter.44.cloned.1.call-start = ((), (), s32[]{:S(2)}) async-start(), calls=%async_computation.34 | async-start | bytes 655360 | tf_op jit(solution)/shard_map/reduce_scatter | solution.py:51
  1099.6 7.1 collective-permute-start.15
  1105.0 64.2 %reduce-scatter.50.cloned.1.call-start = ((), (), s32[]{:S(2)}) async-start(), calls=%async_computation.37 | async-start | bytes 655360 | tf_op jit(solution)/shard_map/reduce_scatter | solution.py:51
  (216 other events, 2904.7 us)
Sparse Core Ops, SparseCore 0:
  379.0 20.6 reduce-scatter.21
  402.4 21.6 reduce-scatter.27
  426.6 21.6 reduce-scatter.33
  481.8 22.0 reduce-scatter.35
  506.7 21.6 reduce-scatter.29
  542.5 22.0 reduce-scatter.23
  651.7 19.8 reduce-scatter.25
  674.8 21.6 reduce-scatter.31
  699.0 21.6 reduce-scatter.37
  784.0 22.1 reduce-scatter.45
  808.6 21.6 reduce-scatter.39
  832.8 21.6 reduce-scatter.51
  918.3 20.3 reduce-scatter.47
  941.2 21.6 reduce-scatter.53
  965.3 21.6 reduce-scatter.41
  989.4 21.8 reduce-scatter.59
  1013.6 21.6 reduce-scatter.61
  1037.8 21.6 reduce-scatter.57
  1098.9 21.8 reduce-scatter.55
  1123.3 21.6 reduce-scatter.43
  1147.5 21.6 reduce-scatter.49
Sparse Core Ops, SparseCore 1:
  545.0 49.6 all-gather.8
  596.5 49.0 all-gather.10
  776.2 72.7 all-reduce.9
where the time goes:
time: 1190 us; the launch traced here: 1180 us
  blocking collectives  478 us (40%)
  waiting for transfers between devices  292 us (25%)
  matrix products  176 us (15%)
  other arithmetic  130 us (11%)
  local copies, waits for them, and re-layouts  54.5 us (5%)
  starting transfers between devices  28.5 us (2%)
  between operations  19.5 us (2%)
    reduce_scatter x21, waiting for transfers between devices, head_total(): lax.psum_scatter(partial_sum.astype(jnp.bfloat16), 'head', scatter_dimens...  157 us
    all_gather x21, blocking collectives, features(): return lax.all_gather(shard_rows, 'head', axis=1, tiled=True)  154 us
    ppermute x24, waiting for transfers between devices, from_partner(): lax.ppermute(value, axis, [(i, i ^ 1 << stride) for i in range(lax.axis_s...  47.9 us
    psum x1, waiting for transfers between devices, shards(): lax.psum(shortened(trained), 'seq')  46.6 us
    all_gather x1, waiting for transfers between devices, shards(): lax.all_gather(ff_out, 'seq', axis=1, tiled=True)  39.2 us
    psum x1, blocking collectives, shards(): lax.psum(shortened(trained), 'seq')  38.7 us
    psum x6, blocking collectives, row_sums(): lax.psum((jnp.sum(left_term, axis=1), jnp.sum(right_term, axis=1)), 'head')  38.5 us
    all_gather x1, blocking collectives, shards(): lax.all_gather(w_query, 'seq', axis=0, tiled=True)  32.6 us
  transfers between devices with their start and end apart: 48, of which 20 were waited for; matrix products, arithmetic and copies ran while one was open for 24% of the time, Pallas kernels for 0%

commit v1 on v0

--- a/solution.py
+++ b/solution.py
@@ -1,6 +1,11 @@
+import functools
+import types
+
 import jax
 import jax.numpy as jnp
 from jax import lax
+from jax.experimental import pallas as pl
+from jax.experimental.pallas import tpu as pltpu
 from jax.sharding import PartitionSpec as P
 
 D = 1024
@@ -444,6 +449,931 @@
     )
 
 
+BF = jnp.bfloat16
+F32 = jnp.float32
+MESH = pl.DeviceIdType.MESH
+NEG = -1000000000.0
+PAD = 32
+LOW = -3.0e38
+
+
+def mm(left, right):
+    return jnp.dot(left, right, preferred_element_type=F32)
+
+
+def mm_nt(left, right):
+    return lax.dot_general(left, right, (((1,), (1,)), ((), ())), preferred_element_type=F32)
+
+
+def flip(matrix):
+    return matrix.astype(F32).T.astype(BF)
+
+
+def lanes(start, size):
+    return pl.ds(pl.multiple_of(start, 128), size)
+
+
+def rows_at(start, size):
+    return pl.ds(pl.multiple_of(start, 16), size)
+
+
+class Links:
+    def __init__(self):
+        self.count = 0
+
+    def take(self, number):
+        first = self.count
+        self.count += number
+        return first
+
+
+def layer_norm(residual):
+    center = residual - jnp.mean(residual, axis=1, keepdims=True)
+    inverse = lax.rsqrt(jnp.mean(center * center, axis=1, keepdims=True) + norm_epsilon)
+    return center * inverse, inverse
+
+
+def layer_norm_back(normed, inverse, upstream):
+    mean_up = jnp.mean(upstream, axis=1, keepdims=True)
+    mean_along = jnp.mean(upstream * normed, axis=1, keepdims=True)
+    return inverse * (upstream - mean_up - normed * mean_along)
+
+
+ROW_WEIGHTS = ("wq", "wk", "wv", "cq", "ck", "cv", "fi")
+COL_WEIGHTS = ("wo", "co", "fo")
+WEIGHT_GROUPS = (("wq", "wk", "wv"), ("ck", "cv"), ("wo", "cq"), ("co", "fi"), ("fo",))
+
+
+def scratch_plan(micro, tok, feat):
+    half = tok // 2
+    row = 4 * tok
+    width = 4 * feat
+    plan = {}
+
+    def add(dtype=BF, **shapes):
+        for name, shape in shapes.items():
+            plan[name] = (shape, dtype)
+
+    square, flat = (width, feat), (feat, width)
+    add(wq=square, wk=square, wv=square, cq=square, ck=square, cv=square, wo=flat, co=flat)
+    add(fi=(width, width))
+    add(fo=(width, width))
+    add(xf=(micro, tok, width))
+    add(mf=(micro, tok, width))
+    add(ct=(micro, half, width))
+    add(F32, ub=(8, width))
+    add(qs=(micro, 3, feat, tok))
+    add(qr=(micro, 3, HD, row))
+    add(q2s=(micro, feat, tok))
+    add(q2r=(micro, HD, row))
+    add(ks=(micro, 2, feat, tok))
+    add(kr=(micro, 2, HD, row))
+    add(os=(micro, HD, row))
+    add(o2s=(micro, HD, row))
+    add(orx=(micro, feat, tok))
+    add(o2r=(micro, feat, tok))
+    add(F32, log1=(micro, 8, row))
+    add(F32, log2=(micro, 8, row))
+    add(csend=(micro, half, width))
+    add(crecv=(micro, half, width))
+    add(xsend=(micro, half, width))
+    add(xrecv=(2, micro, half, width))
+    add(F32, own=(micro, half, width))
+    whole, part, single = (micro, tok, width), (micro, half, width), (micro, half, 1)
+    add(b1=whole, b2=whole, z3=whole, d2=whole, d1=whole)
+    add(F32, h1=part, h2=part, dr=part, r1=single, r2=single)
+    add(slope=(micro, tok, width))
+    add(act=(tok, width))
+    add(eact=(micro, tok, 128))
+    add(eslope=(micro, tok, 128))
+    add(outx=(micro, half, feat))
+    add(outr=(micro, half, feat))
+    add(F32, gacc=(256, width))
+    add(F32, bias=(8, width))
+    add(dos=(micro, feat, tok))
+    add(dor=(micro, HD, row))
+    add(dqs=(micro, 3, HD, row))
+    add(dqr=(micro, 3, feat, tok))
+    add(fs=(micro, 2, tok, feat))
+    add(fr=(micro, 2, tok, feat))
+    add(F32, fown=(micro, 2, tok, feat))
+    add(fx=(micro, tok, feat))
+    add(fxr=(2, micro, tok, feat))
+    add(gs=(128, width))
+    add(gr=(224, width))
+    add(gfin=(256, width))
+    add(F32, bsend=(4, 8, width))
+    add(F32, brecv=(4, 8, width))
+    add(F32, pacc=(2, PAD, 128))
+    add(F32, prcv=(2, PAD, 128))
+    add(F32, pg=(4, 2, PAD, 128))
+    add(F32, pre=(2, 2, PAD, HD))
+    add(F32, st=(row, tok))
+    add(pb=(row, tok))
+    upright = (row, HD)
+    add(kn=upright, vn=upright, qn=upright, dn=upright)
+    add(F32, dka=upright, dva=upright)
+    return plan
+
+
+N_SEMS = 560
+INPUT_NAMES = tuple(dict(
+    x=0, mem=0, slen=0, wq_in=0, wk_in=0, wv_in=0, wo_in=0, cq_in=0, ck_in=0, cv_in=0, co_in=0, fi_in=0, fo_in=0,
+    ps=0, pc=0, ad=0, db=0, au=0, ub_in=0, cot=0,
+))
+OUTPUT_NAMES = tuple(dict(out=0, ig=0, mg=0, psg=0, pcg=0, adg=0, dbg=0, aug=0, ubg=0))
+
+
+def layer_kernel(names, *refs):
+    g = types.SimpleNamespace(**dict(zip(names, refs)))
+    send_sem, recv_sem = refs[len(names):]
+    micro, tok, feat = g.x.shape
+    half = tok // 2
+    width = 4 * feat
+    row_len = 4 * tok
+
+    s = lax.axis_index("seq")
+    h = lax.axis_index("head")
+    core = lax.rem(h, 2)
+    xpos = lax.div(h, 2)
+    z2 = lax.div(s, 4)
+    j = lax.rem(s, 4)
+    y = lax.rem(s, 2)
+    z1 = lax.div(j, 2)
+    sib = h + 1 - 2 * core
+    xpeer = h + 2 - 4 * xpos
+    diag = sib + 2 - 4 * xpos
+
+    def slot(d):
+        py = y if d % 2 == 0 else 1 - y
+        pz = z1 if d < 2 else 1 - z1
+        return 2 * pz + py
+
+    def row_peer(d):
+        return 4 * z2 + slot(d)
+
+    s1, s2, s4 = row_peer(1), row_peer(2), s + 4 - 8 * z2
+    s6 = 4 * (1 - z2) + slot(2)
+
+    barrier = pltpu.get_barrier_semaphore()
+    partners = [(s, sib), (s, xpeer), (s, diag), (s1, h), (s2, h), (row_peer(3), h), (s4, h)]
+    for partner in partners:
+        pl.semaphore_signal(barrier, inc=1, device_id=partner, device_id_type=MESH)
+    pl.semaphore_wait(barrier, len(partners))
+
+    links = Links()
+
+    def copy(src, dst, number, device):
+        return pltpu.make_async_remote_copy(
+            src_ref=src, dst_ref=dst, send_sem=send_sem.at[number], recv_sem=recv_sem.at[number],
+            device_id=device, device_id_type=MESH,
+        )
+
+    def start(copies):
+        for one in copies:
+            one.start()
+
+    def wait(copies):
+        for one in copies:
+            one.wait()
+
+    def each(body):
+        def step(mb, carry):
+            body(mb)
+            return carry
+        lax.fori_loop(0, micro, step, 0)
+
+    def chunk(name, index):
+        size = getattr(g, name + "_in").shape[0 if name in ROW_WEIGHTS else 1]
+        if name in ROW_WEIGHTS:
+            return getattr(g, name).at[rows_at(index * size, size), :]
+        return getattr(g, name).at[:, lanes(index * size, size)]
+
+    weight_sem = {name: links.take(7) for group in WEIGHT_GROUPS for name in group}
+    rounds = ((s4, (s,), 0), (s2, (s, s4), 1), (s1, (s, s4, s2, s6), 3))
+
+    def weight_copies(group, step):
+        peer, owned, offset = rounds[step]
+        made = []
+        for name in WEIGHT_GROUPS[group]:
+            for i, index in enumerate(owned):
+                made.append(copy(chunk(name, index), chunk(name, index), weight_sem[name] + offset + i, (peer, h)))
+        return made
+
+    def weights(group, step):
+        if step > 0:
+            wait(weight_copies(group, step - 1))
+        if step < 3:
+            start(weight_copies(group, step))
+
+    x_sem, m_sem = links.take(3 * micro), links.take(3 * micro)
+
+    def gather_copy(source, full, base, k, mb):
+        number = base + k * micro + mb
+        own = full.at[mb, :, lanes(h * feat, feat)]
+        if k == 0:
+            return copy(source.at[mb], own, number, (s, xpeer))
+        if k == 1:
+            return copy(source.at[mb], own, number, (s, sib))
+        passed = full.at[mb, :, lanes(xpeer * feat, feat)]
+        return copy(passed, passed, number, (s, sib))
+
+    c_sem = links.take(3 * micro)
+
+    def cot_copies(mb):
+        made = []
+        for k, (peer, token_half) in enumerate(((xpeer, core), (sib, 1 - core), (diag, 1 - core))):
+            made.append(copy(
+                g.cot.at[mb, rows_at(token_half * half, half), :],
+                g.ct.at[mb, :, lanes(h * feat, feat)],
+                c_sem + k * micro + mb, (s, peer)))
+        return made
+
+    def stamp(name):
+        if name in ROW_WEIGHTS:
+            size = getattr(g, name + "_in").shape[0]
+            getattr(g, name)[rows_at(s * size, size), :] = getattr(g, name + "_in")[...]
+        else:
+            size = getattr(g, name + "_in").shape[1]
+            getattr(g, name)[:, lanes(s * size, size)] = getattr(g, name + "_in")[...]
+
+    for name in WEIGHT_GROUPS[0]:
+        stamp(name)
+    weights(0, 0)
+    for mb in range(micro):
+        start([gather_copy(g.x, g.xf, x_sem, k, mb) for k in (0, 1)])
+    for group in WEIGHT_GROUPS[1:]:
+        for name in group:
+            stamp(name)
+    weights(1, 0)
+
+    def place(mb):
+        g.xf[mb, :, lanes(h * feat, feat)] = g.x[mb]
+        g.mf[mb, :, lanes(h * feat, feat)] = g.mem[mb]
+        g.ct[mb, :, lanes(h * feat, feat)] = g.cot[mb, rows_at(core * half, half), :]
+
+    each(place)
+
+    u_sem = links.take(3)
+    g.ub[:, lanes(h * feat, feat)] = jnp.broadcast_to(g.ub_in[...].astype(F32), (8, feat))
+    own_bias = g.ub.at[:, lanes(h * feat, feat)]
+    bias_copies = [copy(own_bias, own_bias, u_sem + k, (s, peer)) for k, peer in enumerate((xpeer, sib, diag))]
+    start(bias_copies)
+
+    for side, given in enumerate((g.ps, g.pc)):
+        for kind in range(2):
+            whole = given[kind].astype(F32)
+            picked = jnp.zeros((whole.shape[0], HD), F32)
+            for i in range(4):
+                picked = jnp.where(j == i, whole[:, i * HD:(i + 1) * HD], picked)
+            g.pre[side, kind] = jnp.zeros((PAD, HD), F32)
+            g.pre[side, kind, 0:whole.shape[0], :] = picked
+    pre_count = g.ps.shape[1]
+    g.pacc[...] = jnp.zeros_like(g.pacc)
+    g.gacc[...] = jnp.zeros_like(g.gacc)
+    g.bias[...] = jnp.zeros_like(g.bias)
+
+    weights(0, 1)
+    weights(1, 1)
+    for mb in range(micro):
+        gather_copy(g.x, g.xf, x_sem, 0, mb).wait()
+        gather_copy(g.x, g.xf, x_sem, 2, mb).start()
+    for mb in range(micro):
+        start([gather_copy(g.mem, g.mf, m_sem, k, mb) for k in (0, 1)])
+    weights(0, 2)
+    weights(2, 0)
+
+    def self_cols(index, part):
+        return index * half if part == 0 else (7 - index) * half
+
+    qkv_sem = links.take(6 * micro)
+
+    def qkv_copies(mb):
+        made = []
+        for d in (1, 2, 3):
+            for part in range(2):
+                made.append(copy(
+                    g.qs.at[mb, :, rows_at(slot(d) * HD, HD), pl.ds(part * half, half)],
+                    g.qr.at[mb, :, :, lanes(self_cols(j, part), half)],
+                    qkv_sem + ((d - 1) * 2 + part) * micro + mb, (row_peer(d), h)))
+        return made
+
+    kv_sem = links.take(3 * micro)
+
+    def kv_copies(mb):
+        return [copy(
+            g.ks.at[mb, :, rows_at(slot(d) * HD, HD), :],
+            g.kr.at[mb, :, :, lanes(j * tok, tok)],
+            kv_sem + (d - 1) * micro + mb, (row_peer(d), h)) for d in (1, 2, 3)]
+
+    q2_sem = links.take(3 * micro)
+    do2_sem = links.take(3 * micro)
+
+    def plain_copies(source, target, base, mb):
+        return [copy(
+            source.at[mb, rows_at(slot(d) * HD, HD), :],
+            target.at[mb, :, lanes(j * tok, tok)],
+            base + (d - 1) * micro + mb, (row_peer(d), h)) for d in (1, 2, 3)]
+
+    do_sem = links.take(6 * micro)
+
+    def do_copies(mb):
+        made = []
+        for d in (1, 2, 3):
+            for part in range(2):
+                made.append(copy(
+                    g.dos.at[mb, rows_at(slot(d) * HD, HD), pl.ds(part * half, half)],
+                    g.dor.at[mb, :, lanes(self_cols(j, part), half)],
+                    do_sem + ((d - 1) * 2 + part) * micro + mb, (row_peer(d), h)))
+        return made
+
+    o_sem = links.take(6 * micro)
+
+    def o_copies(mb):
+        made = []
+        for d in (1, 2, 3):
+            for part in range(2):
+                made.append(copy(
+                    g.os.at[mb, :, lanes(self_cols(slot(d), part), half)],
+                    g.orx.at[mb, rows_at(j * HD, HD), pl.ds(part * half, half)],
+                    o_sem + ((d - 1) * 2 + part) * micro + mb, (row_peer(d), h)))
+        return made
+
+    o2_sem = links.take(3 * micro)
+
+    def o2_copies(mb):
+        return [copy(
+            g.o2s.at[mb, :, lanes(slot(d) * tok, tok)],
+            g.o2r.at[mb, rows_at(j * HD, HD), :],
+            o2_sem + (d - 1) * micro + mb, (row_peer(d), h)) for d in (1, 2, 3)]
+
+    d2_sem = links.take(3 * micro)
+
+    def d2_copies(mb):
+        return [copy(
+            g.dqs.at[mb, :, :, lanes(slot(d) * tok, tok)],
+            g.dqr.at[mb, :, rows_at(j * HD, HD), :],
+            d2_sem + (d - 1) * micro + mb, (row_peer(d), h)) for d in (1, 2, 3)]
+
+    d1_sem = links.take(6 * micro)
+
+    def d1_copies(mb):
+        made = []
+        for d in (1, 2, 3):
+            for part in range(2):
+                made.append(copy(
+                    g.dqs.at[mb, :, :, lanes(self_cols(slot(d), part), half)],
+                    g.dqr.at[mb, :, rows_at(j * HD, HD), pl.ds(part * half, half)],
+                    d1_sem + ((d - 1) * 2 + part) * micro + mb, (row_peer(d), h)))
+        return made
+
+    core_sem = [links.take(micro) for _ in range(5)]
+    x_sum_sem = [links.take(micro) for _ in range(5)]
+    full_sem = [links.take(micro) for _ in range(5)]
+    fulls = [g.b1, g.b2, g.z3, g.d2, g.d1]
+
+    def core_copy(k, mb):
+        return copy(g.csend.at[mb], g.crecv.at[mb], core_sem[k] + mb, (s, sib))
+
+    def x_copy(k, mb):
+        return copy(g.xsend.at[mb], g.xrecv.at[k % 2, mb], x_sum_sem[k] + mb, (s, xpeer))
+
+    def full_copy(k, mb):
+        mine = fulls[k].at[mb, rows_at(core * half, half), :]
+        return copy(mine, mine, full_sem[k] + mb, (s, sib))
+
+    def put_partial(k, mb, columns):
+        for n in range(4):
+            at = slice(n * feat, (n + 1) * feat)
+            part = columns(n)
+            top, bottom = part[:half], part[half:]
+            g.csend[mb, :, at] = jnp.where(core == 0, bottom, top).astype(BF)
+            g.own[mb, :, at] = jnp.where(core == 0, top, bottom)
+        core_copy(k, mb).start()
+
+    def sum_cores(k, mb):
+        core_copy(k, mb).wait()
+        g.xsend[mb] = (g.own[mb] + g.crecv[mb].astype(F32)).astype(BF)
+        x_copy(k, mb).start()
+
+    def summed(k, mb):
+        x_copy(k, mb).wait()
+        return g.xsend[mb].astype(F32) + g.xrecv[k % 2, mb].astype(F32)
+
+    def put_full(k, mb, value):
+        fulls[k][mb, rows_at(core * half, half), :] = value.astype(BF)
+        full_copy(k, mb).start()
+
+    f_core_sem = [links.take(micro) for _ in range(2)]
+    f_x_sem = [links.take(micro) for _ in range(2)]
+
+    def f_core_copy(k, mb):
+        return copy(g.fs.at[mb], g.fr.at[mb], f_core_sem[k] + mb, (s, sib))
+
+    def f_x_copy(k, mb):
+        return copy(g.fx.at[mb], g.fxr.at[k, mb], f_x_sem[k] + mb, (s, xpeer))
+
+    def put_features(k, mb, quarter_of):
+        for side in range(2):
+            g.fs[mb, side] = quarter_of((2 * side + 1 - core) * feat).astype(BF)
+        f_core_copy(k, mb).start()
+        for side in range(2):
+            g.fown[mb, side] = quarter_of((2 * side + core) * feat)
+
+    def sum_features(k, mb):
+        f_core_copy(k, mb).wait()
+        g.fown[mb] += g.fr[mb].astype(F32)
+        g.fx[mb] = g.fown[mb, 1 - xpos].astype(BF)
+        f_x_copy(k, mb).start()
+
+    def summed_features(k, mb):
+        f_x_copy(k, mb).wait()
+        return g.fown[mb, xpos] + g.fxr[k, mb].astype(F32)
+
+    def masks(causal, length, base):
+        keys = lax.broadcasted_iota(jnp.int32, (tok, tok), 0)
+        if causal:
+            return keys <= lax.broadcasted_iota(jnp.int32, (tok, tok), 1)
+        return keys < length - base
+
+    def attend(mb, query, keys, values, side, mixed, log_ref, length):
+        causal = side == 0
+        g.kn[...] = flip(keys[...])
+        pre_keys = g.pre[side, 0].astype(BF)
+        pre_values_t = g.pre[side, 1].T.astype(BF)
+        pre_row = lax.broadcasted_iota(jnp.int32, (PAD, tok), 0)
+
+        def chunk_at(c, blocks, at):
+            queries = query[:, at]
+            pre_scores = jnp.where(pre_row < pre_count, mm(pre_keys, queries), LOW)
+            top = jnp.max(pre_scores, axis=0, keepdims=True)
+            for b in range(blocks):
+                scores = mm(g.kn[b * tok:(b + 1) * tok, :], queries)
+                if not causal or b == blocks - 1:
+                    scores = jnp.where(masks(causal, length, b * tok), scores, NEG)
+                g.st[b * tok:(b + 1) * tok, :] = scores
+                top = jnp.maximum(top, jnp.max(scores, axis=0, keepdims=True))
+            pre_weights = jnp.exp(pre_scores - top)
+            total = jnp.sum(pre_weights, axis=0, keepdims=True)
+            for b in range(blocks):
+                weight = jnp.exp(g.st[b * tok:(b + 1) * tok, :] - top)
+                total = total + jnp.sum(weight, axis=0, keepdims=True)
+                g.pb[b * tok:(b + 1) * tok, :] = weight.astype(BF)
+            blend = mm(values[:, 0:blocks * tok], g.pb[0:blocks * tok, :]) + mm(pre_values_t, pre_weights.astype(BF))
+            mixed[:, at] = (blend / total).astype(BF)
+            log_ref[0:1, at] = top + jnp.log(total)
+
+        if causal:
+            for c in range(4):
+                chunk_at(c, c + 1, pl.ds(c * tok, tok))
+        else:
+            def step(c, carry):
+                chunk_at(c, 4, lanes(c * tok, tok))
+                return carry
+            lax.fori_loop(0, 4, step, 0)
+
+    def attend_back(mb, query, keys, values, side, mixed, log_ref, length, grad):
+        causal = side == 0
+        g.kn[...] = flip(keys[...])
+        g.vn[...] = flip(values[...])
+        g.qn[...] = flip(query[...])
+        g.dn[...] = flip(grad[...])
+        g.dka[...] = jnp.zeros_like(g.dka)
+        g.dva[...] = jnp.zeros_like(g.dva)
+        pre_keys = g.pre[side, 0].astype(BF)
+        pre_keys_t = g.pre[side, 0].T.astype(BF)
+        pre_values = g.pre[side, 1].astype(BF)
+        pre_row = lax.broadcasted_iota(jnp.int32, (PAD, tok), 0)
+
+        def chunk_at(c, blocks, at, down):
+            queries, grads = query[:, at], grad[:, at]
+            queries_n, grads_n = g.qn[down, :], g.dn[down, :]
+            logs = log_ref[0:1, at]
+            delta = jnp.sum(mixed[:, at].astype(F32) * grads.astype(F32), axis=0, keepdims=True)
+            pre_weights = jnp.where(pre_row < pre_count, jnp.exp(mm(pre_keys, queries) - logs), 0.0)
+            pre_grad = (pre_weights * (mm(pre_values, grads) - delta)).astype(BF)
+            total = mm(pre_keys_t, pre_grad)
+            g.pacc[side, :, 0:HD] += mm(pre_grad, queries_n)
+            g.pacc[side, :, HD:2 * HD] += mm(pre_weights.astype(BF), grads_n)
+            for b in range(blocks):
+                here = slice(b * tok, (b + 1) * tok)
+                weight = jnp.exp(mm(g.kn[here, :], queries) - logs)
+                if not causal or b == blocks - 1:
+                    weight = jnp.where(masks(causal, length, b * tok), weight, 0.0)
+                score_grad = (weight * (mm(g.vn[here, :], grads) - delta)).astype(BF)
+                g.dka[here, :] += mm(score_grad, queries_n)
+                g.dva[here, :] += mm(weight.astype(BF), grads_n)
+                total = total + mm(keys[:, here], score_grad)
+            g.dqs[mb, 0, :, at] = total.astype(BF)
+
+        if causal:
+            for c in range(4):
+                chunk_at(c, c + 1, pl.ds(c * tok, tok), pl.ds(c * tok, tok))
+        else:
+            def step(c, carry):
+                chunk_at(c, 4, lanes(c * tok, tok), rows_at(c * tok, tok))
+                return carry
+            lax.fori_loop(0, 4, step, 0)
+        g.dqs[mb, 1] = g.dka[...].T.astype(BF)
+        g.dqs[mb, 2] = g.dva[...].T.astype(BF)
+
+    def length_of(mb):
+        return g.slen[mb, z2]
+
+    def project_self(mb):
+        gather_copy(g.x, g.xf, x_sem, 1, mb).wait()
+        gather_copy(g.x, g.xf, x_sem, 2, mb).wait()
+        for k, name in enumerate(("wq", "wk", "wv")):
+            value = mm(g.xf[mb], getattr(g, name)[...])
+            if k == 0:
+                value = value * 0.125
+            g.qs[mb, k] = value.T.astype(BF)
+        start(qkv_copies(mb))
+        for part in range(2):
+            g.qr[mb, :, :, lanes(self_cols(j, part), half)] = (
+                g.qs[mb, :, rows_at(j * HD, HD), part * half:(part + 1) * half])
+
+    weights(0, 3)
+    weights(1, 2)
+    weights(2, 1)
+    each(project_self)
+    for mb in range(micro):
+        gather_copy(g.mem, g.mf, m_sem, 0, mb).wait()
+        gather_copy(g.mem, g.mf, m_sem, 2, mb).start()
+    weights(2, 2)
+    weights(3, 0)
+
+    def self_forward(mb):
+        wait(qkv_copies(mb))
+        attend(mb, g.qr.at[mb, 0], g.qr.at[mb, 1], g.qr.at[mb, 2], 0, g.os.at[mb], g.log1.at[mb], None)
+        start(o_copies(mb))
+        for part in range(2):
+            g.orx[mb, rows_at(j * HD, HD), part * half:(part + 1) * half] = (
+                g.os[mb, :, lanes(self_cols(j, part), half)])
+
+    each(self_forward)
+    weights(1, 3)
+    weights(3, 1)
+    weights(4, 0)
+
+    def project_memory(mb):
+        gather_copy(g.mem, g.mf, m_sem, 1, mb).wait()
+        gather_copy(g.mem, g.mf, m_sem, 2, mb).wait()
+        for k, name in enumerate(("ck", "cv")):
+            g.ks[mb, k] = mm(g.mf[mb], getattr(g, name)[...]).T.astype(BF)
+        start(kv_copies(mb))
+        g.kr[mb, :, :, lanes(j * tok, tok)] = g.ks[mb, :, rows_at(j * HD, HD), :]
+
+    each(project_memory)
+    weights(2, 3)
+
+    def self_out(mb):
+        wait(o_copies(mb))
+        blend = flip(g.orx[mb])
+        put_partial(0, mb, lambda n: mm(blend, g.wo[:, n * feat:(n + 1) * feat]))
+
+    each(self_out)
+    weights(3, 2)
+    weights(4, 1)
+    each(lambda mb: sum_cores(0, mb))
+    weights(4, 2)
+
+    def norm_one(mb):
+        residual = g.xf[mb, rows_at(core * half, half), :].astype(F32) + summed(0, mb)
+        normed, inverse = layer_norm(residual)
+        g.h1[mb] = normed
+        g.r1[mb] = inverse
+        put_full(0, mb, normed)
+
+    each(norm_one)
+
+    def project_cross(mb):
+        full_copy(0, mb).wait()
+        value = mm(g.b1[mb], g.cq[...]) * 0.125
+        g.q2s[mb] = value.T.astype(BF)
+        start(plain_copies(g.q2s, g.q2r, q2_sem, mb))
+        g.q2r[mb, :, lanes(j * tok, tok)] = g.q2s[mb, rows_at(j * HD, HD), :]
+
+    each(project_cross)
+
+    def cross_forward(mb):
+        wait(kv_copies(mb))
+        wait(plain_copies(g.q2s, g.q2r, q2_sem, mb))
+        attend(mb, g.q2r.at[mb], g.kr.at[mb, 0], g.kr.at[mb, 1], 1, g.o2s.at[mb], g.log2.at[mb], length_of(mb))
+        start(o2_copies(mb))
+        g.o2r[mb, rows_at(j * HD, HD), :] = g.o2s[mb, :, lanes(j * tok, tok)]
+
+    each(cross_forward)
+    each(lambda mb: start(cot_copies(mb)))
+    weights(3, 3)
+
+    def cross_out(mb):
+        wait(o2_copies(mb))
+        blend = flip(g.o2r[mb])
+        put_partial(1, mb, lambda n: mm(blend, g.co[:, n * feat:(n + 1) * feat]))
+
+    each(cross_out)
+    each(lambda mb: sum_cores(1, mb))
+
+    def norm_two(mb):
+        normed, inverse = layer_norm(g.h1[mb] + summed(1, mb))
+        g.h2[mb] = normed
+        g.r2[mb] = inverse
+        put_full(1, mb, normed)
+
+    each(norm_two)
+    weights(4, 3)
+
+    def gelu_pair(value):
+        phi = 0.5 * (1.0 + lax.erf(value * 0.7071067811865476))
+        slope = phi + value * jnp.exp(-0.5 * value * value) * 0.3989422804014327
+        return value * phi, slope
+
+    def feed_forward(mb):
+        full_copy(1, mb).wait()
+        rows = g.b2[mb]
+        for n in range(4):
+            at = slice(n * feat, (n + 1) * feat)
+            active, slope = gelu_pair(mm(rows, g.fi[:, at]))
+            g.act[:, at] = active.astype(BF)
+            g.slope[mb, :, at] = slope.astype(BF)
+        active, slope = gelu_pair(mm(rows, g.ad[...]) + g.db[...].astype(F32))
+        active = active.astype(BF)
+        g.eact[mb] = active
+        g.eslope[mb] = slope.astype(BF)
+
+        def columns(n):
+            at = slice(n * feat, (n + 1) * feat)
+            return mm(g.act[...], g.fo[:, at]) + 4.0 * mm(active, g.au[:, at])
+
+        put_partial(2, mb, columns)
+
+    each(feed_forward)
+    each(lambda mb: sum_cores(2, mb))
+    wait(bias_copies)
+    out_sem = links.take(micro)
+
+    def out_copy(mb):
+        return copy(g.outx.at[mb], g.outr.at[mb], out_sem + mb, (s, sib))
+
+    def norm_three(mb):
+        residual = g.h2[mb] + summed(2, mb) + 4.0 * g.ub[0:1, :]
+        normed, inverse = layer_norm(residual)
+        g.own[mb] = normed
+        mine, other = lanes(h * feat, feat), lanes(sib * feat, feat)
+        g.out[mb, rows_at(core * half, half), :] = g.own[mb, :, mine].astype(BF)
+        g.outx[mb] = g.own[mb, :, other].astype(BF)
+        out_copy(mb).start()
+        wait(cot_copies(mb))
+        back = layer_norm_back(normed, inverse, g.ct[mb].astype(F32))
+        g.dr[mb] = back
+        put_full(2, mb, back)
+        g.bias[0:1, :] += 4.0 * jnp.sum(back, axis=0, keepdims=True)
+
+    each(norm_three)
+
+    def feed_back(mb):
+        full_copy(2, mb).wait()
+        up = g.z3[mb]
+        for n in range(4):
+            at = slice(n * feat, (n + 1) * feat)
+            g.act[:, at] = (mm_nt(up, g.fo[at, :]) * g.slope[mb, :, at].astype(F32)).astype(BF)
+        adapt = (4.0 * mm_nt(up, g.au[...]) * g.eslope[mb].astype(F32)).astype(BF)
+
+        def columns(n):
+            at = slice(n * feat, (n + 1) * feat)
+            return mm_nt(g.act[...], g.fi[at, :]) + mm_nt(adapt, g.ad[at, :])
+
+        put_partial(3, mb, columns)
+        g.gacc[0:128, :] += 4.0 * mm(flip(g.eact[mb]), up)
+        g.gacc[128:256, :] += mm(flip(adapt), g.b2[mb])
+        g.bias[1:2, 0:128] += jnp.sum(adapt.astype(F32), axis=0, keepdims=True)
+
+    each(feed_back)
+    each(lambda mb: sum_cores(3, mb))
+
+    grad_sem = links.take(6)
+    first_half, first_other = y * 128, (1 - y) * 128
+    quarter, quarter_other = first_half + z1 * 64, first_half + (1 - z1) * 64
+    eighth, eighth_other = quarter + z2 * 32, quarter + (1 - z2) * 32
+    halving = ((s1, first_half, first_other, 128, 0), (s2, quarter, quarter_other, 64, 128), (s4, eighth, eighth_other, 32, 192))
+
+    def grad_down(step):
+        peer, keep, give, size, offset = halving[step]
+        return copy(g.gs.at[pl.ds(0, size), :], g.gr.at[pl.ds(offset, size), :], grad_sem + step, (peer, h))
+
+    def grad_down_start(step):
+        peer, keep, give, size, offset = halving[step]
+        g.gs[0:size, :] = g.gacc[rows_at(give, size), :].astype(BF)
+        grad_down(step).start()
+
+    def grad_down_end(step):
+        peer, keep, give, size, offset = halving[step]
+        grad_down(step).wait()
+        g.gacc[rows_at(keep, size), :] += g.gr[offset:offset + size, :].astype(F32)
+
+    doubling = ((s4, eighth, 32), (s2, quarter, 64), (s1, first_half, 128))
+
+    def grad_up(step):
+        peer, keep, size = doubling[step]
+        mine = g.gfin.at[rows_at(keep, size), :]
+        return copy(mine, mine, grad_sem + 3 + step, (peer, h))
+
+    bias_sem = links.take(4)
+
+    def bias_copy(step):
+        peer = ((s, sib), (s1, h), (s2, h), (s4, h))[step]
+        return copy(g.bsend.at[step], g.brecv.at[step], bias_sem + step, peer)
+
+    def bias_start(step):
+        g.bsend[step] = g.bias[...]
+        bias_copy(step).start()
+
+    def bias_end(step):
+        bias_copy(step).wait()
+        if step == 0:
+            g.bias[0:1, :] += g.brecv[step, 0:1, :]
+        else:
+            g.bias[...] += g.brecv[step]
+
+    bias_start(0)
+    grad_down_start(0)
+
+    def norm_two_back(mb):
+        upstream = g.dr[mb] + summed(3, mb)
+        back = layer_norm_back(g.h2[mb], g.r2[mb], upstream)
+        g.dr[mb] = back
+        put_full(3, mb, back)
+
+    each(norm_two_back)
+    bias_end(0)
+    bias_start(1)
+
+    def cross_grad(mb):
+        full_copy(3, mb).wait()
+        g.dos[mb] = mm_nt(g.co[...], g.d2[mb]).astype(BF)
+        start(plain_copies(g.dos, g.dor, do2_sem, mb))
+        g.dor[mb, :, lanes(j * tok, tok)] = g.dos[mb, rows_at(j * HD, HD), :]
+
+    each(cross_grad)
+    grad_down_end(0)
+    grad_down_start(1)
+
+    def cross_backward(mb):
+        wait(plain_copies(g.dos, g.dor, do2_sem, mb))
+        attend_back(mb, g.q2r.at[mb], g.kr.at[mb, 0], g.kr.at[mb, 1], 1, g.o2s.at[mb], g.log2.at[mb],
+                    length_of(mb), g.dor.at[mb])
+        start(d2_copies(mb))
+        g.dqr[mb, :, rows_at(j * HD, HD), :] = g.dqs[mb, :, :, lanes(j * tok, tok)]
+
+    each(cross_backward)
+    bias_end(1)
+    bias_start(2)
+    grad_down_end(1)
+    grad_down_start(2)
+
+    def cross_project_back(mb):
+        wait(d2_copies(mb))
+        queries = (g.dqr[mb, 0].astype(F32) * 0.125).T.astype(BF)
+        put_partial(4, mb, lambda n: mm_nt(queries, g.cq[n * feat:(n + 1) * feat, :]))
+        keys, values = flip(g.dqr[mb, 1]), flip(g.dqr[mb, 2])
+        put_features(0, mb, lambda at: mm_nt(keys, g.ck[rows_at(at, feat), :]) + mm_nt(values, g.cv[rows_at(at, feat), :]))
+
+    each(cross_project_back)
+
+    def sum_both(mb):
+        sum_cores(4, mb)
+        sum_features(0, mb)
+
+    each(sum_both)
+    grad_down_end(2)
+    g.gfin[rows_at(eighth, 32), :] = g.gacc[rows_at(eighth, 32), :].astype(BF)
+    grad_up(0).start()
+    bias_end(2)
+    bias_start(3)
+
+    def norm_one_back(mb):
+        upstream = g.dr[mb] + summed(4, mb)
+        back = layer_norm_back(g.h1[mb], g.r1[mb], upstream)
+        put_full(4, mb, back)
+
+    each(norm_one_back)
+
+    def self_grad(mb):
+        full_copy(4, mb).wait()
+        g.dos[mb] = mm_nt(g.wo[...], g.d1[mb]).astype(BF)
+        start(do_copies(mb))
+        for part in range(2):
+            g.dor[mb, :, lanes(self_cols(j, part), half)] = g.dos[mb, rows_at(j * HD, HD), part * half:(part + 1) * half]
+
+    each(self_grad)
+    grad_up(0).wait()
+    grad_up(1).start()
+
+    def memory_out(mb):
+        g.mg[mb] = summed_features(0, mb).astype(BF)
+
+    each(memory_out)
+
+    def self_backward(mb):
+        wait(do_copies(mb))
+        attend_back(mb, g.qr.at[mb, 0], g.qr.at[mb, 1], g.qr.at[mb, 2], 0, g.os.at[mb], g.log1.at[mb], None,
+                    g.dor.at[mb])
+        start(d1_copies(mb))
+        for part in range(2):
+            g.dqr[mb, :, rows_at(j * HD, HD), part * half:(part + 1) * half] = (
+                g.dqs[mb, :, :, lanes(self_cols(j, part), half)])
+
+    each(self_backward)
+
+    pre_sem = links.take(4)
+    pre_sum = copy(g.pacc, g.prcv, pre_sem, (s4, h))
+    pre_sum.start()
+    grad_up(1).wait()
+    grad_up(2).start()
+    bias_end(3)
+
+    def self_project_back(mb):
+        wait(d1_copies(mb))
+        queries = (g.dqr[mb, 0].astype(F32) * 0.125).T.astype(BF)
+        keys, values = flip(g.dqr[mb, 1]), flip(g.dqr[mb, 2])
+
+        def quarter_of(at):
+            here = rows_at(at, feat)
+            return mm_nt(queries, g.wq[here, :]) + mm_nt(keys, g.wk[here, :]) + mm_nt(values, g.wv[here, :])
+
+        put_features(1, mb, quarter_of)
+
+    each(self_project_back)
+    pre_sum.wait()
+    g.pg[j] = g.pacc[...] + g.prcv[...]
+    pre_share = [copy(g.pg.at[j], g.pg.at[j], pre_sem + d, (row_peer(d), h)) for d in (1, 2, 3)]
+    start(pre_share)
+    each(lambda mb: sum_features(1, mb))
+
+    def out_rest(mb):
+        out_copy(mb).wait()
+        g.out[mb, rows_at((1 - core) * half, half), :] = g.outr[mb]
+
+    each(out_rest)
+    grad_up(2).wait()
+    g.aug[...] = g.gfin[0:128, :].astype(F32)
+    g.adg[...] = g.gfin[128:256, :].astype(F32).T
+    g.dbg[...] = g.bias[1:2, 0:128]
+    g.ubg[...] = g.bias[0:1, lanes(h * feat, feat)]
+    wait(pre_share)
+    for side, target in enumerate((g.psg, g.pcg)):
+        for kind in range(2):
+            for i in range(4):
+                target[kind, :, i * HD:(i + 1) * HD] = g.pg[i, side, 0:pre_count, kind * HD:(kind + 1) * HD]
+
+    def input_out(mb):
+        g.ig[mb] = (g.d1[mb, :, lanes(h * feat, feat)].astype(F32) + summed_features(1, mb)).astype(BF)
+
+    each(input_out)
+    assert links.count <= N_SEMS
+
+
+def fused_shards(*args):
+    inputs = args[0]
+    micro, tok, feat = inputs.shape
+    width = 4 * feat
+    args = list(args)
+    args[16] = args[16].reshape(1, -1)
+    args[18] = args[18].reshape(1, -1)
+    plan = scratch_plan(micro, tok, feat)
+    names = INPUT_NAMES + OUTPUT_NAMES + tuple(plan)
+    pre = args[13].shape
+    shapes = (
+        ((micro, tok, feat), BF), ((micro, tok, feat), BF), ((micro, tok, feat), BF),
+        (pre, F32), (pre, F32), (args[15].shape, F32), (args[16].shape, F32), (args[17].shape, F32), (args[18].shape, F32),
+    )
+    specs = [pl.BlockSpec(memory_space=pltpu.VMEM) for _ in args]
+    specs[2] = pl.BlockSpec(memory_space=pltpu.SMEM)
+    results = pl.pallas_call(
+        functools.partial(layer_kernel, names),
+        out_shape=[jax.ShapeDtypeStruct(shape, dtype) for shape, dtype in shapes],
+        in_specs=specs,
+        out_specs=[pl.BlockSpec(memory_space=pltpu.VMEM) for _ in shapes],
+        scratch_shapes=[pltpu.VMEM(shape, dtype) for shape, dtype in plan.values()]
+        + [pltpu.SemaphoreType.DMA((N_SEMS,)), pltpu.SemaphoreType.DMA((N_SEMS,))],
+        compiler_params=pltpu.CompilerParams(
+            collective_id=0, has_side_effects=True, vmem_limit_bytes=VMEM_BYTES),
+        name="decoder_layer",
+    )(*args)
+    results = list(results)
+    results[6] = results[6].reshape(-1)
+    results[8] = results[8].reshape(-1)
+    return tuple(results)
+
+
+VMEM_BYTES = 63 * 1024 * 1024
+
+
+def fits_fused(mesh):
+    return dict(mesh.shape) == {"seq": 8, "head": 4}
+
+
 def solution(mesh):
     in_specs = (
         P(None, "seq", "head"),
@@ -478,4 +1408,5 @@
         P("head", None),
         P("head"),
     )
-    return jax.shard_map(shards, mesh=mesh, in_specs=in_specs, out_specs=out_specs, check_vma=False)
+    body = fused_shards if fits_fused(mesh) else shards
+    return jax.shard_map(body, mesh=mesh, in_specs=in_specs, out_specs=out_specs, check_vma=False)

time: 1190 us -> 345 us (0.29)
  blocking collectives: 478 us -> 0 us
  Pallas kernels: 0 us -> 331 us
  waiting for transfers between devices: 292 us -> 0 us
  matrix products: 176 us -> 0 us
  other arithmetic: 130 us -> 0 us
  local copies, waits for them, and re-layouts: 54.5 us -> 13 us
  starting transfers between devices: 28.5 us -> 0 us
  between operations: 19.5 us -> 0.68 us
    all_gather x29 -> x0, blocking collectives: 401 us -> none  [the longest x21 154 us: features(): return lax.all_gather(shard_rows, 'head', axis=1, tiled=True)]
    pallas_call x0 -> x1, Pallas kernels: none -> 331 us  [fused_shards(): pl.pallas_call(functools.partial(layer_kernel, names), out_shape=[jax.Sha...]
    dot_general x147 -> x0, matrix products: 176 us -> none  [the longest x3 15.6 us: shards(): jnp.einsum('tf,df->td', grad_hidden, hidden_in, preferred_element_type=jn...]
    reduce_scatter x21 -> x0, waiting for transfers between devices: 157 us -> none  [head_total(): lax.psum_scatter(partial_sum.astype(jnp.bfloat16), 'head', scatter_dimens...]
    psum x7 -> x0, blocking collectives: 77.1 us -> none  [the longest x1 38.7 us: shards(): lax.psum(shortened(trained), 'seq')]
    convert_element_type x47 -> x0, other arithmetic: 51.3 us -> none  [the longest x4 17.3 us: attend_backward(): (weights * (grad_weights - row_delta[:, :, None])).astype(jnp.bfloat16)]
    ppermute x24 -> x0, waiting for transfers between devices: 47.9 us -> none  [from_partner(): lax.ppermute(value, axis, [(i, i ^ 1 << stride) for i in range(lax.axis_s...]
    psum x1 -> x0, waiting for transfers between devices: 46.6 us -> none  [shards(): lax.psum(shortened(trained), 'seq')]
  transfers between devices with their start and end apart: 48 -> 0, of which waited for: 20 -> 0; matrix products, arithmetic and copies ran while one was open for 24% -> 0% of each run, Pallas kernels for 0% -> 0%
where the time goes in v1:
time: 345 us
  Pallas kernels  331 us (96%)
  local copies, waits for them, and re-layouts  13 us (4%)
    pallas_call x1, Pallas kernels, fused_shards(): pl.pallas_call(functools.partial(layer_kernel, names), out_shape=[jax.Sha...  331 us
    unnamed x32, local copies, waits for them, and re-layouts  12.5 us

profile of v1, /device:TPU:0, one launch (start us, length us, event | category | flops | bytes accessed | tf_op | source)
XLA Modules:
  0.0 344.9 jit_solution(707814929308139371)
XLA Ops:
  0.6 0.0 copy-start.8
  0.7 0.6 copy-done.8
  1.3 0.0 copy-start.6
  1.3 0.6 reshape.31.refs_18_
  1.9 0.1 copy-done.6
  2.0 0.7 copy.29.refs_2_
  2.6 0.0 copy-start.5
  2.6 1.4 copy.30.refs_13_
  4.0 0.0 copy-done.5
  4.0 0.6 copy.31.refs_14_
  4.6 331.2 %decoder_layer.1 = (bf16[3,256,256]{2,1,0:T(8,128)(2,1)}, bf16[3,256,256]{2,1,0:T(8,128)(2,1)}, bf16[3,256,256]{2,1,0:T(8,128)(2,1)}, f32[2,30,256]{2,1,0:T(8,12...) custom-call(bf16[3,256,256]{2,1,0:T(8,128)(2,1)} %refs_0_.1, ...), custom_call_target="tpu_custom_call" | custom-call | tf_op jit(solution)/shard_map/decoder_layer/pallas_call | solution.py:1353
  335.8 0.0 copy-start.4
  335.8 1.5 copy.32
  337.4 0.0 copy-done.4
  337.4 0.7 copy.33
  338.1 0.0 copy-start.3
  338.1 1.8 copy.41
  339.9 0.0 copy-done.3
  339.9 0.0 copy-start.2
  339.9 0.7 copy.42
  340.6 0.4 copy-done.2
  341.0 0.0 copy-start.1
  341.0 0.7 copy.43
  341.8 0.4 copy-done.1
  342.2 0.0 copy-start.9
  342.2 0.0 copy-start
  342.2 0.8 copy.44
  343.0 0.0 copy-done.9
  343.0 0.5 copy.45
  343.5 0.0 copy-done
  343.5 0.0 copy-start.7
  343.5 0.8 copy.46
  344.3 0.0 copy-done.7
  344.3 0.6 copy.47
Async XLA Ops:
  0.6 0.7 copy-start.8
  1.3 0.7 copy-start.6
  2.6 1.4 copy-start.5
  335.8 1.6 copy-start.4
  338.1 1.8 copy-start.3
  339.9 1.1 copy-start.2
  341.0 1.2 copy-start.1
  342.2 0.8 copy-start.9
  342.2 1.3 copy-start
  343.5 0.8 copy-start.7
